TPU v7x, 512 devices: a whole 4x4x16 slice. The times are simulated.
512 devices in a mesh: blk: 32 (over x, z_lo), rep: 16 (over z_hi, y, core).
Axes of the slice: x: 4, y: 4, z: 16 (z_hi: 2, z_lo: 8; z = z_hi * 8 + z_lo), core: 2. Of those that a mesh axis runs over, the one named last changes fastest.
Arguments:
- features: bfloat16 [65536, 128], P(('blk', 'rep')), may hold values from -6 to 6
- weight: bfloat16 [128, 128], replicated, may hold values from -0.5 to 0.5
- adjacency: bfloat16 [32, 16, 2, 32, 2, 128, 128], P('blk', 'rep'), may hold values from 0 to 0.019042969
- row_tiles: int32 [32, 16, 2, 32, 2], P('blk', 'rep'), may hold values from 0 to 15
- live_counts: int32 [32, 16, 2, 32], P('blk', 'rep'), may hold values from 0 to 2, as said below
- upstream: bfloat16 [65536, 128], P(('blk', 'rep')), may hold values from -6 to 6
Outputs:
- hidden: bfloat16 [65536, 128], P(('blk', 'rep'))
- input_grad: bfloat16 [65536, 128], P(('blk', 'rep'))
- weight_grad: float32 [128, 128], replicated
Inputs may be any that keep to these rules, and one draw needn't show every extreme that they name: `live_counts`: in every device's own set (s = 0) at least one bucket is full; row blocks differ in load, and a device's second set holds tiles of the row block before its own.
All inputs are finite; a program needn't handle non-finite values.
Results may differ from a plain program's by a relative error of at most 0.03.
Values may be sent and summed in bfloat16 or wider, within the bound.
A program may use at most 64 MiB of HBM per device.

v0:
```python
import jax
import jax.numpy as jnp
from jax import lax
from jax.sharding import PartitionSpec as P


def passed_along(value, axis, steps):
    count = lax.axis_size(axis)
    pairs = [(source, (source + steps) % count) for source in range(count)]
    return lax.ppermute(value, axis, pairs)


def silu_slope(values):
    squashed = jax.nn.sigmoid(values)
    return squashed * (1.0 + values * (1.0 - squashed))


def send_back(values):
    return passed_along(values.astype(jnp.bfloat16), "blk", -1).astype(values.dtype)


def send_ahead(values):
    return passed_along(values, "blk", 1)


def local(features, weight, adjacency, row_tiles, live_counts, upstream):
    tile_side = features.shape[0]
    width = features.shape[1]
    groups = lax.axis_size("rep")
    my_tiles = adjacency[0, 0]
    slot_count = my_tiles.shape[2]
    alive_slots = (
        jnp.arange(slot_count, dtype=jnp.int32)[None, None, :] < live_counts[0, 0][:, :, None]
    )
    chooser = (row_tiles[0, 0][..., None] == jnp.arange(groups, dtype=jnp.int32)) & alive_slots[
        ..., None
    ]
    chooser_narrow = chooser.astype(jnp.bfloat16)
    mixed = jnp.dot(features, weight, preferred_element_type=jnp.float32).astype(jnp.bfloat16)
    shard_rows = lax.all_gather(mixed, "blk", axis=0, tiled=True)
    blocks_here = shard_rows.shape[0] // tile_side
    part_tiles = my_tiles
    part_pick = chooser_narrow
    stacked = shard_rows.reshape(blocks_here, tile_side, width)
    products = jnp.einsum(
        "snkij,njf->snkif", part_tiles, stacked, preferred_element_type=jnp.float32
    )
    upper = products.astype(jnp.bfloat16)
    lower = (products - upper.astype(jnp.float32)).astype(jnp.bfloat16)
    routed = jnp.einsum("snkt,snkif->stif", part_pick, upper, preferred_element_type=jnp.float32)
    routed = routed + jnp.einsum(
        "snkt,snkif->stif", part_pick, lower, preferred_element_type=jnp.float32
    )
    owned = routed[0].reshape(groups * tile_side, width)
    helped = routed[1].reshape(groups * tile_side, width)
    summed = lax.psum_scatter(
        (owned + send_back(helped)).astype(jnp.bfloat16), "rep", scatter_dimension=0, tiled=True
    ).astype(jnp.float32)
    hidden = jax.nn.silu(summed).astype(jnp.bfloat16)
    slope = (upstream.astype(jnp.float32) * silu_slope(summed)).astype(jnp.bfloat16)
    slope_rows = lax.all_gather(slope, "rep", axis=0, tiled=True)
    slope_help = send_ahead(slope_rows)
    slope_sets = jnp.stack(
        [slope_rows.reshape(groups, tile_side, width), slope_help.reshape(groups, tile_side, width)]
    )
    part_tiles = my_tiles
    part_pick = chooser_narrow
    chosen = jnp.einsum(
        "snkt,stif->snkif", part_pick, slope_sets, preferred_element_type=jnp.float32
    ).astype(jnp.bfloat16)
    terms = jnp.einsum("snkij,snkif->njf", part_tiles, chosen, preferred_element_type=jnp.float32)
    column_sum = lax.psum_scatter(
        terms.reshape(tile_side * lax.axis_size("blk"), width).astype(jnp.bfloat16),
        "blk",
        scatter_dimension=0,
        tiled=True,
    )
    input_grad = jnp.dot(column_sum, weight.T, preferred_element_type=jnp.float32).astype(
        jnp.bfloat16
    )
    local_grad = lax.dot_general(
        features, column_sum, (((0,), (0,)), ((), ())), preferred_element_type=jnp.float32
    )
    weight_grad = lax.psum(local_grad, ("blk", "rep"))
    return (hidden, input_grad, weight_grad)


def solution(mesh):
    in_specs = (
        P(("blk", "rep"), None),
        P(),
        P("blk", "rep", None, None, None, None, None),
        P("blk", "rep", None, None, None),
        P("blk", "rep", None, None),
        P(("blk", "rep"), None),
    )
    out_specs = (P(("blk", "rep"), None), P(("blk", "rep"), None), P())
    return jax.shard_map(local, mesh=mesh, in_specs=in_specs, out_specs=out_specs, check_vma=False)
```

profile of v0, /device:TPU:1, one launch (start us, length us, event | category | flops | bytes accessed | tf_op | source)
XLA Modules:
  0.0 1142.1 jit_solution(4715023134440035094)
XLA Ops:
  7.2 0.0 copy-start
  7.2 0.0 all-gather.2.cloned.1.call-start
  7.2 0.7 copy-done
  7.9 1.5 convolution_convert_fusion.1
  9.4 0.0 all-gather.2.cloned.1.call-update
  9.5 0.0 reduce-scatter.3.cloned.1.call-start
  9.5 0.7 iota_compare_fusion.1
  10.2 206.8 %all-gather.2.cloned.1.call-done = bf16[4096,128]{1,0:T(8,128)(2,1)} async-done(((bf16[128,128]{1,0:T(8,128)(2,1)}), bf16[4096,128]{1,0:T(8,128)(2,1)}) %all-gather.2.cloned.1.call-update) | async-done | bytes 1048592 | tf_op jit(solution)/shard_map/all_gather | solution.py:40
  217.0 7.3 fusion
  224.2 7.9 copy.17
  232.1 0.0 copy-start.5
  232.1 8.0 copy.18
  240.1 0.0 copy-start.1
  240.1 0.0 copy-done.5
  240.1 3.1 fusion.26
  243.2 0.4 copy-done.1
  243.6 0.7 bitcast_add_fusion
  244.3 0.1 slice.12
  244.4 0.0 copy-start.4
  244.4 0.1 copy.20
  244.5 11.2 collective-permute-start
  255.7 0.1 slice.9
  255.8 0.3 copy.19
  256.1 5.7 collective-permute-done
  261.8 0.9 fusion.10
  262.7 0.0 reduce-scatter.3.cloned.1.call-update
  262.7 0.0 reduce-scatter.5.cloned.1.call-start
  262.8 121.5 %reduce-scatter.3.cloned.1.call-done = bf16[128,128]{1,0:T(8,128)(2,1)} async-done(((bf16[2048,128]{1,0:T(8,128)(2,1)}), bf16[128,128]{1,0:T(8,128)(2,1)}) %reduce-scatter.3.cloned.1.call-update) | async-done | bytes 32784 | tf_op jit(solution)/shard_map/reduce_scatter | solution.py:56
  384.3 0.0 copy-done.4
  384.3 0.0 copy-start.2
  384.3 1.6 fusion.20
  385.9 39.1 %all_gather.7 = bf16[2048,128]{1,0:T(8,128)(2,1)S(1)} all-gather(bf16[128,128]{1,0:T(8,128)(2,1)S(1)} %get-tuple-element.11), channel_id=1, replica_groups=mesh['blk'=32,'rep'=16] {'rep'}, dimensions={0}, use_global_device_ids=true | all-gather | bytes 557056 | tf_op jit(solution)/shard_map/all_gather | solution.py:61
  425.0 1.9 collective-permute-start.1
  426.9 22.1 %collective-permute-done.1 = bf16[2048,128]{1,0:T(8,128)(2,1)S(1)} collective-permute-done((bf16[2048,128]{1,0:T(8,128)(2,1)S(1)}, bf16[2048,128]{1,0:T(8,128)(2,1)S(1)}, u32[]{:S(2)}, u32[]{:S(2)}) %collective-permute-start.1) | collective-permute-done | bytes 524320 | tf_op jit(solution)/shard_map/ppermute | solution.py:10
  449.0 0.1 maximum_bitcast_fusion
  449.1 1.3 fusion.11
  450.4 0.0 copy-done.2
  450.4 0.0 copy-start.3
  450.4 6.3 bitcast_convert_fusion.1
  456.7 0.0 reduce-scatter.5.cloned.1.call-update
  456.7 0.0 all-reduce.2.cloned.1.call-start
  456.8 214.2 %reduce-scatter.5.cloned.1.call-done = bf16[128,128]{1,0:T(8,128)(2,1)} async-done(((bf16[4096,128]{1,0:T(8,128)(2,1)}), bf16[128,128]{1,0:T(8,128)(2,1)}) %reduce-scatter.5.cloned.1.call-update) | async-done | bytes 32784 | tf_op jit(solution)/shard_map/reduce_scatter | solution.py:72
  671.0 1.6 convolution_bitcast_fusion
  672.5 0.0 all-reduce.2.cloned.1.call-update
  672.6 0.0 copy-done.3
  672.6 1.5 convolution_convert_fusion
  674.1 459.9 %all-reduce.2.cloned.1.call-done = f32[128,128]{0,1:T(8,128)} async-done(((f32[128,128]{0,1:T(8,128)}), f32[128,128]{0,1:T(8,128)}) %all-reduce.2.cloned.1.call-update) | async-done | bytes 65552 | tf_op jit(solution)/shard_map/psum | solution.py:84
  1134.0 1.6 copy.22
Async XLA Ops:
  7.2 0.8 copy-start
  7.2 209.8 %all-gather.2.cloned.1.call-start = ((), (), s32[]{:S(2)}) async-start(), calls=%async_computation.2 | async-start | bytes 1081344 | tf_op jit(solution)/shard_map/all_gather | solution.py:40
  9.5 374.8 %reduce-scatter.3.cloned.1.call-start = ((), (), s32[]{:S(2)}) async-start(), calls=%async_computation.3 | async-start | bytes 557056 | tf_op jit(solution)/shard_map/reduce_scatter | solution.py:56
  232.1 8.0 copy-start.5
  240.1 3.4 copy-start.1
  244.4 139.9 %copy-start.4 = (bf16[128,128]{1,0:T(8,128)(2,1)S(1)}, bf16[128,128]{1,0:T(8,128)(2,1)}, u32[]{:S(2)}) copy-start(bf16[128,128]{1,0:T(8,128)(2,1)} %param.11) | copy-start | bytes 98308
  244.5 17.3 %collective-permute-start = (bf16[2048,128]{1,0:T(8,128)(2,1)S(1)}, bf16[2048,128]{1,0:T(8,128)(2,1)S(1)}, u32[]{:S(2)}, u32[]{:S(2)}) collective-permute-start(bf16[2048,128]{1,0:T(8,128)(2,1)S(1)} %bitcast.66), channel_id=1, source_target_pairs={{0,496},{16,0},{32,16},{48,32},{64,48},{80,64},{96,80},{112,96},{1... | collective-permute-start | bytes 1572872 | tf_op jit(solution)/shard_map/ppermute | solution.py:10
  262.7 408.2 %reduce-scatter.5.cloned.1.call-start = ((), (), s32[]{:S(2)}) async-start(), calls=%async_computation.4 | async-start | bytes 1081344 | tf_op jit(solution)/shard_map/reduce_scatter | solution.py:72
  384.3 66.1 %copy-start.2 = (bf16[1,1,2,32,2,128,128]{6,5,4,3,2,1,0:T(8,128)(2,1)S(1)}, bf16[1,1,2,32,2,128,128]{6,5,4,3,2,1,0:T(8,128)(2,1)}, u32[]{:S(2)}) copy-start(bf16[1,1,2,32,2,128,128]{6,5,4,3,2,1,0:T(8,128)(2,1)} %param.8) | copy-start | bytes 12582916
  425.0 24.0 %collective-permute-start.1 = (bf16[2048,128]{1,0:T(8,128)(2,1)S(1)}, bf16[2048,128]{1,0:T(8,128)(2,1)S(1)}, u32[]{:S(2)}, u32[]{:S(2)}) collective-permute-start(bf16[2048,128]{1,0:T(8,128)(2,1)S(1)} %all_gather.7), channel_id=1, source_target_pairs={{0,16},{16,32},{32,48},{48,64},{64,80},{80,96},{96,112},{112,128},... | collective-permute-start | bytes 1572872 | tf_op jit(solution)/shard_map/ppermute | solution.py:10
  450.4 222.2 %copy-start.3 = (bf16[128,128]{1,0:T(8,128)(2,1)S(1)}, bf16[128,128]{1,0:T(8,128)(2,1)}, u32[]{:S(2)}) copy-start(bf16[128,128]{1,0:T(8,128)(2,1)} %param.7) | copy-start | bytes 98308
  456.7 677.3 %all-reduce.2.cloned.1.call-start = ((), (), s32[]{:S(2)}) async-start(), calls=%async_computation.5 | async-start | bytes 131072 | tf_op jit(solution)/shard_map/psum | solution.py:84
Sparse Core Ops, SparseCore 0:
  10.7 206.2 all-gather.1
  262.9 121.3 reduce-scatter.2
  456.8 214.0 reduce-scatter.4
  676.8 457.1 all-reduce.1
where the time goes:
time: 1140 us
  waiting for transfers between devices  1030 us (90%)
  blocking collectives  39.1 us (3%)
  matrix products  23.2 us (2%)
  local copies, waits for them, and re-layouts  19.2 us (2%)
  between operations  13.9 us (1%)
  starting transfers between devices  13.2 us (1%)
    psum x1, waiting for transfers between devices, local(): weight_grad = lax.psum(local_grad, ('blk', 'rep'))  460 us
    reduce_scatter x1, waiting for transfers between devices, local(): lax.psum_scatter(terms.reshape(tile_side * lax.axis_size('blk'), width).a...  214 us
    all_gather x1, waiting for transfers between devices, local(): shard_rows = lax.all_gather(mixed, 'blk', axis=0, tiled=True)  207 us
    reduce_scatter x1, waiting for transfers between devices, local(): lax.psum_scatter((owned + send_back(helped)).astype(jnp.bfloat16), 'rep',...  122 us
    all_gather x1, blocking collectives, local(): slope_rows = lax.all_gather(slope, 'rep', axis=0, tiled=True)  39.1 us
    ppermute x2, waiting for transfers between devices, passed_along(): return lax.ppermute(value, axis, pairs)  27.7 us
  transfers between devices with their start and end apart: 6, of which 6 were waited for; matrix products, arithmetic and copies ran while one was open for 0% of the time, Pallas kernels for 0%

commit v1 on v0

v1 whole, which is shorter than its diff:
```python
import functools

import jax
import jax.numpy as jnp
from jax import lax
from jax.experimental import pallas as pl
from jax.experimental.pallas import tpu as pltpu
from jax.sharding import PartitionSpec as P

MESH = pl.DeviceIdType.MESH
X, ZL, ZH, Y = 4, 8, 2, 4
T = 128


def dot(a, b):
    return jnp.dot(a, b, preferred_element_type=jnp.float32)


def kernel(
    table,
    feat,
    weight,
    up,
    adj_hbm,
    hidden,
    input_grad,
    weight_grad,
    adj,
    feats,
    sums,
    c1_out,
    c1_in,
    c2_out,
    c2_in,
    part,
    c3_out,
    c3_in,
    slopes,
    terms,
    gx_in,
    gz_out,
    gz_in,
    wg_out,
    h1_in,
    h2_buf,
    h3_buf,
    wg_all,
    adj_sem,
    az_s,
    az_r,
    ax_s,
    ax_r,
    c1_s,
    c1_r,
    c2_s,
    c2_r,
    c3_s,
    c3_r,
    e1_s,
    e1_r,
    e2_s,
    e2_r,
    e3_s,
    e3_r,
    gx_s,
    gx_r,
    gz_s,
    gz_r,
    h1_s,
    h1_r,
    h2_s,
    h2_r,
    h3_s,
    h3_r,
    h4_s,
    h4_r,
):
    BLK, REP = X * ZL, ZH * Y * 2
    SL = 2 * BLK
    f32, bf16 = jnp.float32, jnp.bfloat16
    b = lax.axis_index("blk")
    r = lax.axis_index("rep")
    x, z = b // ZL, b % ZL
    zh, y, core = r // (2 * Y), (r // 2) % Y, r % 2
    ozh = (zh + 1) % ZH
    b_up, b_dn = (b + 1) % BLK, (b + BLK - 1) % BLK

    def at_z(d):
        return (x * ZL + (z + d) % ZL, r)

    def at_x(d):
        return (((x + d) % X) * ZL + z, r)

    def rep_of(h, v, c):
        return (h * Y + v) * 2 + c

    def at_y(d):
        return (b, rep_of(zh, (y + d) % Y, core))

    sib = (b, rep_of(zh, y, 1 - core))
    r_oz = rep_of(ozh, y, core)

    def rc(src, dst, ss, rs, dev):
        return pltpu.make_async_remote_copy(
            src_ref=src, dst_ref=dst, send_sem=ss, recv_sem=rs, device_id=dev, device_id_type=MESH
        )

    load = pltpu.make_async_copy(adj_hbm, adj, adj_sem)
    load.start()

    bar = pltpu.get_barrier_semaphore()

    def greet(dev):
        pl.semaphore_signal(bar, inc=1, device_id=dev, device_id_type=MESH)

    for d in range(1, ZL):
        greet(at_z(d))
    for d in range(1, X):
        greet(at_x(d))
    for dev in ((b_up, r), (b_dn, r), (b_up, r_oz), (b_dn, r_oz)):
        greet(dev)
    for d in range(1, REP):
        greet((b, (r + d) % REP))
    pl.semaphore_wait(bar, (ZL - 1) + (X - 1) + 4 + (REP - 1))

    sends = []

    def go(copy):
        copy.start()
        sends.append(copy)
        return copy

    for d in range(1, ZL):
        go(rc(feat, feats.at[b], az_s.at[d], az_r.at[d], at_z(d)))
    for e in range(1, X):
        go(rc(feat, feats.at[b], ax_s.at[e, 0], ax_r.at[e, 0], at_x(e)))
    feats[b] = feat[...]
    sums[2 * SL] = jnp.zeros((T, T), f32)
    slopes[2 * REP] = jnp.zeros((T, T), bf16)
    for d in range(1, ZL):
        n = x * ZL + (z + ZL - d) % ZL
        rc(feat, feats.at[n], az_s.at[d], az_r.at[d], at_z(d)).wait_recv()
        for e in range(1, X):
            go(rc(feats.at[n], feats.at[n], ax_s.at[e, d], ax_r.at[e, d], at_x(e)))
    for d in range(0, ZL):
        for e in range(1, X):
            n = ((x + X - e) % X) * ZL + (z + ZL - d) % ZL
            rc(feat, feats.at[n], ax_s.at[e, d], ax_r.at[e, d], at_x(e)).wait_recv()
    load.wait()

    w = weight[...]

    def forward(n, carry):
        mixed = dot(feats[n], w).astype(bf16)
        for s in range(2):
            q = s * SL + 2 * n
            a = adj[pl.ds(q, 2)].reshape(2 * T, T)
            prod = dot(a, mixed)
            sums[q] = prod[:T] + sums[table[q]]
            sums[q + 1] = prod[T:] + sums[table[q + 1]]
        return carry

    lax.fori_loop(0, BLK, forward, 0)

    def routed(s, t):
        return sums[table[2 * SL + s * REP + t]]

    order = tuple(range(1, Y)) + (0,)
    for d in order:
        yy = (y + d) % Y
        for s in range(2):
            for h in range(ZH):
                c1_out[d, s * ZH + h] = routed(s, rep_of(h, yy, 1 - core)).astype(bf16)
        go(rc(c1_out.at[d], c1_in.at[d], c1_s.at[d], c1_r.at[d], sib))
    for d in order:
        yy = (y + d) % Y
        rc(c1_out.at[d], c1_in.at[d], c1_s.at[d], c1_r.at[d], sib).wait_recv()
        for s in range(2):
            for h in range(ZH):
                both = routed(s, rep_of(h, yy, core)) + c1_in[d, s * ZH + h].astype(f32)
                if d:
                    c2_out[d, s * ZH + h] = both.astype(bf16)
                else:
                    part[s * ZH + h] = both
        if d:
            go(rc(c2_out.at[d], c2_in.at[d], c2_s.at[d], c2_r.at[d], at_y(d)))
    for d in range(1, Y):
        rc(c2_out.at[d], c2_in.at[d], c2_s.at[d], c2_r.at[d], at_y(d)).wait_recv()
    for i in range(2 * ZH):
        total = part[i]
        for d in range(1, Y):
            total = total + c2_in[d, i].astype(f32)
        part[i] = total
    c3_to = ((b, r_oz), (b_dn, r_oz), (b_dn, r))
    for i, pick in enumerate((ozh, ZH + ozh, ZH + zh)):
        c3_out[i] = part[pick].astype(bf16)
        go(rc(c3_out.at[i], c3_in.at[i], c3_s.at[i], c3_r.at[i], c3_to[i]))
    summed = part[zh]
    for i in range(3):
        rc(c3_out.at[i], c3_in.at[i], c3_s.at[i], c3_r.at[i], c3_to[i]).wait_recv()
        summed = summed + c3_in[i].astype(f32)

    sig = jax.nn.sigmoid(summed)
    slope = up[...].astype(f32) * (sig * (1.0 + summed * (1.0 - sig)))

    def place(s, h, v, c):
        return ((c * Y + v) * 2 + s) * ZH + h

    mine, helps = place(0, zh, y, core), place(1, zh, y, core)
    slopes[mine] = slope.T.astype(bf16)
    own = slopes.at[mine]
    e1 = (
        (slopes.at[mine], (b, r_oz)),
        (slopes.at[helps], (b_up, r_oz)),
        (slopes.at[helps], (b_up, r)),
    )
    for i, (dst, dev) in enumerate(e1):
        go(rc(own, dst, e1_s.at[i], e1_r.at[i], dev))
    hidden[...] = (summed * sig).astype(bf16)
    for i, (dst, dev) in enumerate(e1):
        rc(own, dst, e1_s.at[i], e1_r.at[i], dev).wait_recv()

    def chunk(v, c):
        return slopes.at[pl.ds((c * Y + v) * 2 * ZH, 2 * ZH)]

    for d in range(1, Y):
        go(rc(chunk(y, core), chunk(y, core), e2_s.at[d], e2_r.at[d], at_y(d)))
    go(rc(chunk(y, core), chunk(y, core), e3_s.at[0], e3_r.at[0], sib))
    for d in range(1, Y):
        v = (y + Y - d) % Y
        rc(chunk(v, core), chunk(v, core), e2_s.at[d], e2_r.at[d], at_y(d)).wait_recv()
        go(rc(chunk(v, core), chunk(v, core), e3_s.at[d], e3_r.at[d], sib))
    for d in range(Y):
        v = (y + Y - d) % Y
        got = chunk(v, 1 - core)
        rc(got, got, e3_s.at[d], e3_r.at[d], sib).wait_recv()

    base = 2 * SL + 2 * REP

    def backward(n, total):
        out = None
        for s in range(2):
            q = s * SL + 2 * n
            lhs = jnp.concatenate(
                [slopes[table[base + q]], slopes[table[base + q + 1]]], axis=1
            )
            term = dot(lhs, adj[pl.ds(q, 2)].reshape(2 * T, T))
            out = term if out is None else out + term
        out = out.astype(bf16)
        terms[n] = out
        return total + dot(out, feats[n])

    total = jnp.zeros((T, T), f32)
    for e in tuple(range(1, X)) + (0,):
        first = ((x + e) % X) * ZL
        total = lax.fori_loop(0, ZL, lambda i, t: backward(first + i, t), total)
        if e:
            go(rc(terms.at[pl.ds(first, ZL)], gx_in.at[e], gx_s.at[e], gx_r.at[e], at_x(e)))

    wg_out[...] = total.reshape(REP, T // REP, T)

    def h1(d):
        q = (r + d) % REP
        return rc(wg_out.at[q], h1_in.at[d], h1_s.at[d], h1_r.at[d], (b, q))

    def loop(lo, hi, body):
        def step(i, c):
            body(i)
            return c

        lax.fori_loop(lo, hi, step, 0)

    loop(1, REP, lambda d: h1(d).start())

    for e in range(1, X):
        rc(gx_in.at[e], gx_in.at[e], gx_s.at[e], gx_r.at[e], at_x(e)).wait_recv()
    kept = None
    for d in tuple(range(1, ZL)) + (0,):
        v = (z + d) % ZL
        s = terms[x * ZL + v].astype(f32)
        for e in range(1, X):
            s = s + gx_in[e, v].astype(f32)
        if d:
            gz_out[d] = s.astype(bf16)
            go(rc(gz_out.at[d], gz_in.at[d], gz_s.at[d], gz_r.at[d], at_z(d)))
        else:
            kept = s

    loop(1, REP, lambda d: h1(d).wait_recv())
    unit = wg_out[r]
    for d in range(1, REP):
        unit = unit + h1_in[d]
    h2_buf[x] = unit
    for e in range(1, X):
        go(rc(h2_buf.at[x], h2_buf.at[x], h2_s.at[e], h2_r.at[e], at_x(e)))
    for e in range(1, X):
        v = (x + X - e) % X
        rc(h2_buf.at[v], h2_buf.at[v], h2_s.at[e], h2_r.at[e], at_x(e)).wait_recv()
    unit = h2_buf[0]
    for e in range(1, X):
        unit = unit + h2_buf[e]
    h3_buf[z] = unit
    for d in range(1, ZL):
        go(rc(h3_buf.at[z], h3_buf.at[z], h3_s.at[d], h3_r.at[d], at_z(d)))

    for d in range(1, ZL):
        rc(gz_out.at[d], gz_in.at[d], gz_s.at[d], gz_r.at[d], at_z(d)).wait_recv()
        kept = kept + gz_in[d].astype(f32)

    for d in range(1, ZL):
        v = (z + ZL - d) % ZL
        rc(h3_buf.at[v], h3_buf.at[v], h3_s.at[d], h3_r.at[d], at_z(d)).wait_recv()
    unit = h3_buf[0]
    for d in range(1, ZL):
        unit = unit + h3_buf[d]
    wg_all[r] = unit

    def h4(d, to):
        q = (r + REP - d) % REP
        slot = wg_all.at[r] if to else wg_all.at[q]
        return rc(slot, slot, h4_s.at[d], h4_r.at[d], (b, (r + d) % REP))

    loop(1, REP, lambda d: h4(d, True).start())

    pulled = kept.T.astype(bf16)
    input_grad[...] = lax.dot_general(
        pulled, w, (((1,), (1,)), ((), ())), preferred_element_type=f32
    ).astype(bf16)

    loop(1, REP, lambda d: h4(d, False).wait_recv())
    weight_grad[...] = wg_all[...].reshape(T, T).T

    for copy in sends:
        copy.wait_send()
    loop(1, REP, lambda d: h1(d).wait_send())
    loop(1, REP, lambda d: h4(d, True).wait_send())


def tables(row_tiles, live_counts, blocks, reps):
    slots = 2 * blocks
    row = row_tiles.reshape(2, slots)
    count = jnp.repeat(live_counts.reshape(2, blocks), 2, axis=1)
    q = jnp.arange(slots, dtype=jnp.int32)
    alive = (q % 2)[None] < count
    key = jnp.where(alive, row, reps)
    want = jnp.concatenate(
        [key, jnp.broadcast_to(jnp.arange(reps, dtype=jnp.int32), (2, reps))], axis=1
    )
    limit = jnp.concatenate([q, jnp.full((reps,), slots, jnp.int32)])
    hit = (
        (key[:, None, :] == want[:, :, None])
        & alive[:, None, :]
        & (q[None, None, :] < limit[None, :, None])
    )
    at = q[None] + slots * jnp.arange(2, dtype=jnp.int32)[:, None]
    found = jnp.max(jnp.where(hit, at[:, None, :], -1), axis=2)
    found = jnp.where(found < 0, 2 * slots, found)
    h, v, c = row // (2 * Y), (row // 2) % Y, row % 2
    s = jnp.arange(2, dtype=jnp.int32)[:, None]
    pos = jnp.where(alive, ((c * Y + v) * 2 + s) * ZH + h, 2 * reps)
    return jnp.concatenate(
        [found[:, :slots].reshape(-1), found[:, slots:].reshape(-1), pos.reshape(-1)]
    )


def local(features, weight, adjacency, row_tiles, live_counts, upstream):
    BLK, REP = X * ZL, ZH * Y * 2
    f32, bf16 = jnp.float32, jnp.bfloat16
    table = tables(row_tiles, live_counts, BLK, REP)
    adj = adjacency.reshape(4 * BLK, T, T)
    vmem = pl.BlockSpec(memory_space=pltpu.VMEM)

    def buf(*dims, dtype=bf16):
        return pltpu.VMEM(dims + (T,), dtype)

    U = T // REP
    dma = pltpu.SemaphoreType.DMA
    scratch = [
        buf(4 * BLK, T),
        buf(BLK, T),
        buf(4 * BLK + 1, T, dtype=f32),
        buf(Y, 2 * ZH, T),
        buf(Y, 2 * ZH, T),
        buf(Y, 2 * ZH, T),
        buf(Y, 2 * ZH, T),
        buf(2 * ZH, T, dtype=f32),
        buf(3, T),
        buf(3, T),
        buf(2 * REP + 1, T),
        buf(BLK, T),
        buf(X, ZL, T),
        buf(ZL, T),
        buf(ZL, T),
        buf(REP, U, dtype=f32),
        buf(REP, U, dtype=f32),
        buf(X, U, dtype=f32),
        buf(ZL, U, dtype=f32),
        buf(REP, U, dtype=f32),
        dma,
        dma((ZL,)),
        dma((ZL,)),
        dma((X, ZL)),
        dma((X, ZL)),
        dma((Y,)),
        dma((Y,)),
        dma((Y,)),
        dma((Y,)),
        dma((3,)),
        dma((3,)),
        dma((3,)),
        dma((3,)),
        dma((Y,)),
        dma((Y,)),
        dma((Y,)),
        dma((Y,)),
        dma((X,)),
        dma((X,)),
        dma((ZL,)),
        dma((ZL,)),
        dma((REP,)),
        dma((REP,)),
        dma((X,)),
        dma((X,)),
        dma((ZL,)),
        dma((ZL,)),
        dma((REP,)),
        dma((REP,)),
    ]
    return pl.pallas_call(
        kernel,
        name="graph_layer",
        out_shape=(
            jax.ShapeDtypeStruct((T, T), bf16),
            jax.ShapeDtypeStruct((T, T), bf16),
            jax.ShapeDtypeStruct((T, T), f32),
        ),
        in_specs=[
            pl.BlockSpec(memory_space=pltpu.SMEM),
            vmem,
            vmem,
            vmem,
            pl.BlockSpec(memory_space=pl.ANY),
        ],
        out_specs=(vmem, vmem, vmem),
        scratch_shapes=scratch,
        compiler_params=pltpu.CompilerParams(
            collective_id=0, has_side_effects=True, vmem_limit_bytes=48 * 1024 * 1024
        ),
    )(table, features, weight, upstream, adj)


def solution(mesh):
    assert mesh.shape["blk"] == X * ZL and mesh.shape["rep"] == ZH * Y * 2
    in_specs = (
        P(("blk", "rep"), None),
        P(),
        P("blk", "rep", None, None, None, None, None),
        P("blk", "rep", None, None, None),
        P("blk", "rep", None, None),
        P(("blk", "rep"), None),
    )
    out_specs = (P(("blk", "rep"), None), P(("blk", "rep"), None), P())
    return jax.shard_map(local, mesh=mesh, in_specs=in_specs, out_specs=out_specs, check_vma=False)
```

time: 1140 us -> 145 us (0.13)
  waiting for transfers between devices: 1030 us -> 0 us
  Pallas kernels: 0 us -> 134 us
  blocking collectives: 39.1 us -> 0 us
  matrix products: 23.2 us -> 0 us
  between operations: 13.9 us -> 0.69 us
  starting transfers between devices: 13.2 us -> 0 us
    psum x1 -> x0, waiting for transfers between devices: 460 us -> none  [local(): weight_grad = lax.psum(local_grad, ('blk', 'rep'))]
    reduce_scatter x2 -> x0, waiting for transfers between devices: 336 us -> none  [the longest x1 214 us: local(): lax.psum_scatter(terms.reshape(tile_side * lax.axis_size('blk'), width).a...]
    all_gather x1 -> x0, waiting for transfers between devices: 207 us -> none  [local(): shard_rows = lax.all_gather(mixed, 'blk', axis=0, tiled=True)]
    pallas_call x0 -> x1, Pallas kernels: none -> 134 us  [local(): pl.pallas_call(kernel, name='graph_layer', out_shape=(jax.ShapeDtypeStruc...]
    all_gather x1 -> x0, blocking collectives: 39.1 us -> none  [local(): slope_rows = lax.all_gather(slope, 'rep', axis=0, tiled=True)]
    ppermute x2 -> x0, waiting for transfers between devices: 27.7 us -> none  [passed_along(): return lax.ppermute(value, axis, pairs)]
    dot_general x8 -> x0, matrix products: 23.2 us -> none  [the longest x1 7.25 us: local(): jnp.einsum('snkij,njf->snkif', part_tiles, stacked, preferred_element_typ...]
    convert_element_type x2 -> x0, local copies, waits for them, and re-layouts: 15.9 us -> none  [the longest x1 7.99 us: local(): lower = (products - upper.astype(jnp.float32)).astype(jnp.bfloat16)]
  transfers between devices with their start and end apart: 6 -> 0, of which waited for: 6 -> 0; matrix products, arithmetic and copies ran while one was open for 0% -> 0% of each run, Pallas kernels for 0% -> 0%
where the time goes in v1:
time: 145 us; the launch traced here: 144 us
  Pallas kernels  134 us (92%)
  local copies, waits for them, and re-layouts  8.75 us (6%)
    pallas_call x1, Pallas kernels, local(): pl.pallas_call(kernel, name='graph_layer', out_shape=(jax.ShapeDtypeStruc...  134 us
    unnamed x12, local copies, waits for them, and re-layouts  7.09 us

profile of v1, /device:TPU:1, one launch (start us, length us, event | category | flops | bytes accessed | tf_op | source)
XLA Modules:
  0.0 144.3 jit_solution(14207675446786294600)
XLA Ops:
  0.7 0.1 lt.72
  0.7 0.1 add.72
  0.8 0.7 iota_compare_fusion
  1.5 0.8 copy.13
  2.3 0.1 reshape.128
  2.4 0.1 reshape.124
  2.5 0.8 broadcast_in_dim.39
  3.3 0.1 reshape.127
  3.4 0.1 reshape.123
  3.6 0.1 broadcast_select_fusion
  3.6 0.1 pad_add_fusion.1
  3.7 0.1 select_reduce_fusion
  3.8 0.1 reshape.125
  3.9 0.1 slice.7
  4.0 0.1 reshape.126
  4.1 0.1 pad_add_fusion.table
  4.2 0.0 copy-start
  4.2 2.2 %copy-done = bf16[1,1,2,32,2,128,128]{6,5,4,3,2,1,0:T(8,128)(2,1)S(1)} copy-done((bf16[1,1,2,32,2,128,128]{6,5,4,3,2,1,0:T(8,128)(2,1)S(1)}, bf16[1,1,2,32,2,128,128]{6,5,4,3,2,1,0:T(8,128)(2,1)}, u32[]{:S(2)}) %copy-start) | copy-done | bytes 4194328
  6.4 0.0 copy-start.1
  6.4 0.8 copy-done.1
  7.1 0.0 copy-start.2
  7.1 0.8 copy-done.2
  7.9 0.0 copy-start.3
  7.9 0.8 copy-done.3
  8.6 133.8 %graph_layer.1 = (bf16[128,128]{1,0:T(8,128)(2,1)S(1)}, bf16[128,128]{1,0:T(8,128)(2,1)S(1)}, f32[128,128]{1,0:T(8,128)S(1)}) custom-call(s32[288]{0:T(512)S(1)} %pad_add_fusion.table, bf16[128,128]{1,0:T(8,128)(2,1)S(1)} %copy-done.1, bf16[128,128]{1,0:T(8,128)(2,1)S(1)} %copy-done.2, bf16[128,128]{1,0:T(8,128)(2,1)S(1)} %copy-done.3, ...), custom_call_target="tpu_custom_call" | custom-call | tf_op jit(solution)/shard_map/graph_layer/pallas_call | solution.py:429
  142.5 0.6 copy.18
  143.1 0.6 copy.19
  143.7 0.6 copy.20
  (7 shorter events, 0.0 us)
Async XLA Ops:
  4.2 2.2 %copy-start = (bf16[1,1,2,32,2,128,128]{6,5,4,3,2,1,0:T(8,128)(2,1)S(1)}, bf16[1,1,2,32,2,128,128]{6,5,4,3,2,1,0:T(8,128)(2,1)}, u32[]{:S(2)}) copy-start(bf16[1,1,2,32,2,128,128]{6,5,4,3,2,1,0:T(8,128)(2,1)} %param.8) | copy-start | bytes 12582916
  6.4 0.8 copy-start.1
  7.1 0.8 copy-start.2
  7.9 0.8 copy-start.3

commit v2 on v1

--- a/solution.py
+++ b/solution.py
@@ -9,6 +9,7 @@
 
 MESH = pl.DeviceIdType.MESH
 X, ZL, ZH, Y = 4, 8, 2, 4
+ZQ = ZL // 2
 T = 128
 
 
@@ -40,7 +41,11 @@
     gx_in,
     gz_out,
     gz_in,
+    gz2_out,
+    gz2_in,
     wg_out,
+    h0_in,
+    halves,
     h1_in,
     h2_buf,
     h3_buf,
@@ -66,6 +71,10 @@
     gx_r,
     gz_s,
     gz_r,
+    gz2_s,
+    gz2_r,
+    h0_s,
+    h0_r,
     h1_s,
     h1_r,
     h2_s,
@@ -74,6 +83,8 @@
     h3_r,
     h4_s,
     h4_r,
+    h5_s,
+    h5_r,
 ):
     BLK, REP = X * ZL, ZH * Y * 2
     SL = 2 * BLK
@@ -113,15 +124,15 @@
     def greet(dev):
         pl.semaphore_signal(bar, inc=1, device_id=dev, device_id_type=MESH)
 
-    for d in range(1, ZL):
-        greet(at_z(d))
+    for i in range(1, ZH * ZL):
+        greet((x * ZL + (z + i % ZL) % ZL, rep_of((zh + i // ZL) % ZH, y, core)))
     for d in range(1, X):
         greet(at_x(d))
-    for dev in ((b_up, r), (b_dn, r), (b_up, r_oz), (b_dn, r_oz)):
+    for d in range(1, Y):
+        greet(at_y(d))
+    for dev in (sib, (b_up, r), (b_dn, r), (b_up, r_oz), (b_dn, r_oz)):
         greet(dev)
-    for d in range(1, REP):
-        greet((b, (r + d) % REP))
-    pl.semaphore_wait(bar, (ZL - 1) + (X - 1) + 4 + (REP - 1))
+    pl.semaphore_wait(bar, (ZH * ZL - 1) + (X - 1) + (Y - 1) + 5)
 
     sends = []
 
@@ -206,38 +217,58 @@
     def place(s, h, v, c):
         return ((c * Y + v) * 2 + s) * ZH + h
 
-    mine, helps = place(0, zh, y, core), place(1, zh, y, core)
-    slopes[mine] = slope.T.astype(bf16)
-    own = slopes.at[mine]
-    e1 = (
-        (slopes.at[mine], (b, r_oz)),
-        (slopes.at[helps], (b_up, r_oz)),
-        (slopes.at[helps], (b_up, r)),
-    )
-    for i, (dst, dev) in enumerate(e1):
-        go(rc(own, dst, e1_s.at[i], e1_r.at[i], dev))
+    kinds = ((0, zh), (1, zh), (0, ozh), (1, ozh))
+
+    def tile(j, v, c):
+        return slopes.at[place(*kinds[j], v, c)]
+
+    slopes[place(0, zh, y, core)] = slope.T.astype(bf16)
+    own, helps = tile(0, y, core), tile(1, y, core)
+    e1 = ((own, (b, r_oz)), (helps, (b_up, r_oz)), (helps, (b_up, r)))
+
+    def e1_copy(i):
+        dst, dev = e1[i]
+        return rc(own, dst, e1_s.at[i], e1_r.at[i], dev)
+
+    def e2_copy(j, d, v):
+        return rc(tile(j, v, core), tile(j, v, core), e2_s.at[j, d], e2_r.at[j, d], at_y(d))
+
+    def e3_copy(j, d, c):
+        got = tile(j, (y + Y - d) % Y, c)
+        return rc(got, got, e3_s.at[j, d], e3_r.at[j, d], sib)
+
+    def spread(j):
+        for d in range(1, Y):
+            go(e2_copy(j, d, y))
+        go(e3_copy(j, 0, core))
+
+    def pass_on(j):
+        for d in range(1, Y):
+            e2_copy(j, d, (y + Y - d) % Y).wait_recv()
+            go(e3_copy(j, d, core))
+
+    for i in range(3):
+        go(e1_copy(i))
+    spread(0)
     hidden[...] = (summed * sig).astype(bf16)
-    for i, (dst, dev) in enumerate(e1):
-        rc(own, dst, e1_s.at[i], e1_r.at[i], dev).wait_recv()
-
-    def chunk(v, c):
-        return slopes.at[pl.ds((c * Y + v) * 2 * ZH, 2 * ZH)]
-
-    for d in range(1, Y):
-        go(rc(chunk(y, core), chunk(y, core), e2_s.at[d], e2_r.at[d], at_y(d)))
-    go(rc(chunk(y, core), chunk(y, core), e3_s.at[0], e3_r.at[0], sib))
-    for d in range(1, Y):
-        v = (y + Y - d) % Y
-        rc(chunk(v, core), chunk(v, core), e2_s.at[d], e2_r.at[d], at_y(d)).wait_recv()
-        go(rc(chunk(v, core), chunk(v, core), e3_s.at[d], e3_r.at[d], sib))
-    for d in range(Y):
-        v = (y + Y - d) % Y
-        got = chunk(v, 1 - core)
-        rc(got, got, e3_s.at[d], e3_r.at[d], sib).wait_recv()
+    e1_copy(2).wait_recv()
+    spread(1)
+    pass_on(0)
+    e1_copy(0).wait_recv()
+    spread(2)
+    e1_copy(1).wait_recv()
+    spread(3)
+    for j in range(1, 4):
+        pass_on(j)
+    for j in range(4):
+        for d in range(Y):
+            e3_copy(j, d, 1 - core).wait_recv()
 
     base = 2 * SL + 2 * REP
-
-    def backward(n, total):
+    half, zq = z // ZQ, z % ZQ
+    ohalf = 1 - half
+
+    def backward(n):
         out = None
         for s in range(2):
             q = s * SL + 2 * n
@@ -248,92 +279,138 @@
             out = term if out is None else out + term
         out = out.astype(bf16)
         terms[n] = out
-        return total + dot(out, feats[n])
+        return dot(out, feats[n])
+
+    def gx_copy(k, e):
+        first = ((x + e) % X) * ZL + (ohalf, half)[k] * ZQ
+        return rc(terms.at[pl.ds(first, ZQ)], gx_in.at[k, e], gx_s.at[k, e], gx_r.at[k, e], at_x(e))
 
     total = jnp.zeros((T, T), f32)
-    for e in tuple(range(1, X)) + (0,):
-        first = ((x + e) % X) * ZL
-        total = lax.fori_loop(0, ZL, lambda i, t: backward(first + i, t), total)
-        if e:
-            go(rc(terms.at[pl.ds(first, ZL)], gx_in.at[e], gx_s.at[e], gx_r.at[e], at_x(e)))
-
-    wg_out[...] = total.reshape(REP, T // REP, T)
-
-    def h1(d):
-        q = (r + d) % REP
-        return rc(wg_out.at[q], h1_in.at[d], h1_s.at[d], h1_r.at[d], (b, q))
-
-    def loop(lo, hi, body):
-        def step(i, c):
-            body(i)
-            return c
-
-        lax.fori_loop(lo, hi, step, 0)
-
-    loop(1, REP, lambda d: h1(d).start())
-
+    for k in range(2):
+        for e in tuple(range(1, X)) + (0,):
+            first = ((x + e) % X) * ZL + (ohalf, half)[k] * ZQ
+            for i in range(ZQ):
+                total = total + backward(first + i)
+            if e:
+                go(gx_copy(k, e))
+
+    U = T // (2 * Y)
+    wg_out[...] = total.reshape(2 * Y, U, T)
+
+    def h0_copy():
+        return rc(wg_out.at[pl.ds((1 - core) * Y, Y)], h0_in, h0_s, h0_r, sib)
+
+    go(h0_copy())
+
+    def gx_sum(k, v):
+        t = terms[x * ZL + (ohalf, half)[k] * ZQ + v].astype(f32)
+        for e in range(1, X):
+            t = t + gx_in[k, e, v].astype(f32)
+        return t
+
+    def gz_copy(k, m):
+        v = (zq + m) % ZQ
+        return rc(
+            gz_out.at[k, m],
+            gz_in.at[k, m],
+            gz_s.at[k, m],
+            gz_r.at[k, m],
+            (x * ZL + half * ZQ + v, r),
+        )
+
+    def gx_wait(k):
+        for e in range(1, X):
+            gx_copy(k, e).wait_recv()
+        for m in range(1, ZQ):
+            gz_out[k, m] = gx_sum(k, (zq + m) % ZQ).astype(bf16)
+            go(gz_copy(k, m))
+        return gx_sum(k, zq)
+
+    def h1_copy(d):
+        return rc(halves.at[(y + d) % Y], h1_in.at[d], h1_s.at[d], h1_r.at[d], at_y(d))
+
+    h0_copy().wait_recv()
+    halves[...] = wg_out[pl.ds(core * Y, Y)] + h0_in[...]
+    for d in range(1, Y):
+        go(h1_copy(d))
+
+    crossing = gx_wait(0)
+
+    zz = zh * ZL + z
+
+    def h2_copy(i, to):
+        h, d = (zh + i // ZL) % ZH, i % ZL
+        v = (z + (d if to else ZL - d)) % ZL
+        slot = h2_buf.at[zz] if to else h2_buf.at[h * ZL + v]
+        dev = (x * ZL + v, rep_of(h, y, core))
+        return rc(slot, slot, h2_s.at[i], h2_r.at[i], dev)
+
+    unit = halves[y]
+    for d in range(1, Y):
+        h1_copy(d).wait_recv()
+        unit = unit + h1_in[d]
+    h2_buf[zz] = unit.astype(bf16)
+    for i in range(1, ZH * ZL):
+        go(h2_copy(i, True))
+
+    kept = gx_wait(1)
+
+    def gz2_copy():
+        return rc(gz2_out, gz2_in, gz2_s, gz2_r, (x * ZL + ohalf * ZQ + zq, r))
+
+    for m in range(1, ZQ):
+        gz_copy(0, m).wait_recv()
+        crossing = crossing + gz_in[0, m].astype(f32)
+    gz2_out[...] = crossing.astype(bf16)
+    go(gz2_copy())
+    for m in range(1, ZQ):
+        gz_copy(1, m).wait_recv()
+        kept = kept + gz_in[1, m].astype(f32)
+
+    def h3_copy(e, v):
+        return rc(h3_buf.at[v], h3_buf.at[v], h3_s.at[e], h3_r.at[e], at_x(e))
+
+    for i in range(1, ZH * ZL):
+        h2_copy(i, False).wait_recv()
+    unit = h2_buf[0].astype(f32)
+    for i in range(1, ZH * ZL):
+        unit = unit + h2_buf[i].astype(f32)
+    h3_buf[x] = unit
     for e in range(1, X):
-        rc(gx_in.at[e], gx_in.at[e], gx_s.at[e], gx_r.at[e], at_x(e)).wait_recv()
-    kept = None
-    for d in tuple(range(1, ZL)) + (0,):
-        v = (z + d) % ZL
-        s = terms[x * ZL + v].astype(f32)
-        for e in range(1, X):
-            s = s + gx_in[e, v].astype(f32)
-        if d:
-            gz_out[d] = s.astype(bf16)
-            go(rc(gz_out.at[d], gz_in.at[d], gz_s.at[d], gz_r.at[d], at_z(d)))
-        else:
-            kept = s
-
-    loop(1, REP, lambda d: h1(d).wait_recv())
-    unit = wg_out[r]
-    for d in range(1, REP):
-        unit = unit + h1_in[d]
-    h2_buf[x] = unit
-    for e in range(1, X):
-        go(rc(h2_buf.at[x], h2_buf.at[x], h2_s.at[e], h2_r.at[e], at_x(e)))
-    for e in range(1, X):
-        v = (x + X - e) % X
-        rc(h2_buf.at[v], h2_buf.at[v], h2_s.at[e], h2_r.at[e], at_x(e)).wait_recv()
-    unit = h2_buf[0]
-    for e in range(1, X):
-        unit = unit + h2_buf[e]
-    h3_buf[z] = unit
-    for d in range(1, ZL):
-        go(rc(h3_buf.at[z], h3_buf.at[z], h3_s.at[d], h3_r.at[d], at_z(d)))
-
-    for d in range(1, ZL):
-        rc(gz_out.at[d], gz_in.at[d], gz_s.at[d], gz_r.at[d], at_z(d)).wait_recv()
-        kept = kept + gz_in[d].astype(f32)
-
-    for d in range(1, ZL):
-        v = (z + ZL - d) % ZL
-        rc(h3_buf.at[v], h3_buf.at[v], h3_s.at[d], h3_r.at[d], at_z(d)).wait_recv()
-    unit = h3_buf[0]
-    for d in range(1, ZL):
-        unit = unit + h3_buf[d]
-    wg_all[r] = unit
-
-    def h4(d, to):
-        q = (r + REP - d) % REP
-        slot = wg_all.at[r] if to else wg_all.at[q]
-        return rc(slot, slot, h4_s.at[d], h4_r.at[d], (b, (r + d) % REP))
-
-    loop(1, REP, lambda d: h4(d, True).start())
-
-    pulled = kept.T.astype(bf16)
+        go(h3_copy(e, x))
+
+    gz2_copy().wait_recv()
+    pulled = (kept + gz2_in[...].astype(f32)).T.astype(bf16)
     input_grad[...] = lax.dot_general(
         pulled, w, (((1,), (1,)), ((), ())), preferred_element_type=f32
     ).astype(bf16)
 
-    loop(1, REP, lambda d: h4(d, False).wait_recv())
+    def h4_copy(d, v):
+        slot = wg_all.at[core * Y + v]
+        return rc(slot, slot, h4_s.at[d], h4_r.at[d], at_y(d))
+
+    def h5_copy(d, c):
+        slot = wg_all.at[c * Y + (y + Y - d) % Y]
+        return rc(slot, slot, h5_s.at[d], h5_r.at[d], sib)
+
+    for e in range(1, X):
+        h3_copy(e, (x + X - e) % X).wait_recv()
+    unit = h3_buf[0]
+    for e in range(1, X):
+        unit = unit + h3_buf[e]
+    wg_all[core * Y + y] = unit
+    for d in range(1, Y):
+        go(h4_copy(d, y))
+    go(h5_copy(0, core))
+    for d in range(1, Y):
+        h4_copy(d, (y + Y - d) % Y).wait_recv()
+        go(h5_copy(d, core))
+    for d in range(Y):
+        h5_copy(d, 1 - core).wait_recv()
     weight_grad[...] = wg_all[...].reshape(T, T).T
 
     for copy in sends:
         copy.wait_send()
-    loop(1, REP, lambda d: h1(d).wait_send())
-    loop(1, REP, lambda d: h4(d, True).wait_send())
 
 
 def tables(row_tiles, live_counts, blocks, reps):
@@ -373,7 +450,7 @@
     def buf(*dims, dtype=bf16):
         return pltpu.VMEM(dims + (T,), dtype)
 
-    U = T // REP
+    U = T // (2 * Y)
     dma = pltpu.SemaphoreType.DMA
     scratch = [
         buf(4 * BLK, T),
@@ -388,14 +465,18 @@
         buf(3, T),
         buf(2 * REP + 1, T),
         buf(BLK, T),
-        buf(X, ZL, T),
-        buf(ZL, T),
-        buf(ZL, T),
-        buf(REP, U, dtype=f32),
-        buf(REP, U, dtype=f32),
+        buf(2, X, ZQ, T),
+        buf(2, ZQ, T),
+        buf(2, ZQ, T),
+        buf(T),
+        buf(T),
+        buf(2 * Y, U, dtype=f32),
+        buf(Y, U, dtype=f32),
+        buf(Y, U, dtype=f32),
+        buf(Y, U, dtype=f32),
+        buf(ZH * ZL, U),
         buf(X, U, dtype=f32),
-        buf(ZL, U, dtype=f32),
-        buf(REP, U, dtype=f32),
+        buf(2 * Y, U, dtype=f32),
         dma,
         dma((ZL,)),
         dma((ZL,)),
@@ -409,22 +490,28 @@
         dma((3,)),
         dma((3,)),
         dma((3,)),
-        dma((Y,)),
-        dma((Y,)),
-        dma((Y,)),
-        dma((Y,)),
+        dma((4, Y)),
+        dma((4, Y)),
+        dma((4, Y)),
+        dma((4, Y)),
+        dma((2, X)),
+        dma((2, X)),
+        dma((2, ZQ)),
+        dma((2, ZQ)),
+        dma,
+        dma,
+        dma,
+        dma,
+        dma((Y,)),
+        dma((Y,)),
+        dma((ZH * ZL,)),
+        dma((ZH * ZL,)),
         dma((X,)),
         dma((X,)),
-        dma((ZL,)),
-        dma((ZL,)),
-        dma((REP,)),
-        dma((REP,)),
-        dma((X,)),
-        dma((X,)),
-        dma((ZL,)),
-        dma((ZL,)),
-        dma((REP,)),
-        dma((REP,)),
+        dma((Y,)),
+        dma((Y,)),
+        dma((Y,)),
+        dma((Y,)),
     ]
     return pl.pallas_call(
         kernel,

time: 145 us -> 124 us (0.86)
  Pallas kernels: 134 us -> 113 us
    pallas_call x1, Pallas kernels: 134 us -> 113 us  [local(): pl.pallas_call(kernel, name='graph_layer', out_shape=(jax.ShapeDtypeStruc...]
where the time goes in v2:
time: 124 us
  Pallas kernels  113 us (91%)
  local copies, waits for them, and re-layouts  8.75 us (7%)
    pallas_call x1, Pallas kernels, local(): pl.pallas_call(kernel, name='graph_layer', out_shape=(jax.ShapeDtypeStruc...  113 us
    unnamed x12, local copies, waits for them, and re-layouts  7.09 us

profile of v2, /device:TPU:1, one launch (start us, length us, event | category | flops | bytes accessed | tf_op | source)
XLA Modules:
  0.0 123.7 jit_solution(8658408991986062239)
XLA Ops:
  0.7 0.1 lt.72
  0.7 0.1 add.72
  0.8 0.7 iota_compare_fusion
  1.5 0.8 copy.13
  2.3 0.1 reshape.128
  2.4 0.1 reshape.124
  2.5 0.8 broadcast_in_dim.39
  3.3 0.1 reshape.127
  3.4 0.1 reshape.123
  3.6 0.1 broadcast_select_fusion
  3.6 0.1 pad_add_fusion.1
  3.7 0.1 select_reduce_fusion
  3.8 0.1 reshape.125
  3.9 0.1 slice.7
  4.0 0.1 reshape.126
  4.1 0.1 pad_add_fusion.table
  4.2 0.0 copy-start
  4.2 2.2 %copy-done = bf16[1,1,2,32,2,128,128]{6,5,4,3,2,1,0:T(8,128)(2,1)S(1)} copy-done((bf16[1,1,2,32,2,128,128]{6,5,4,3,2,1,0:T(8,128)(2,1)S(1)}, bf16[1,1,2,32,2,128,128]{6,5,4,3,2,1,0:T(8,128)(2,1)}, u32[]{:S(2)}) %copy-start) | copy-done | bytes 4194328
  6.4 0.0 copy-start.1
  6.4 0.8 copy-done.1
  7.1 0.0 copy-start.2
  7.1 0.8 copy-done.2
  7.9 0.0 copy-start.3
  7.9 0.8 copy-done.3
  8.6 113.2 %graph_layer.1 = (bf16[128,128]{1,0:T(8,128)(2,1)S(1)}, bf16[128,128]{1,0:T(8,128)(2,1)S(1)}, f32[128,128]{1,0:T(8,128)S(1)}) custom-call(s32[288]{0:T(512)S(1)} %pad_add_fusion.table, bf16[128,128]{1,0:T(8,128)(2,1)S(1)} %copy-done.1, bf16[128,128]{1,0:T(8,128)(2,1)S(1)} %copy-done.2, bf16[128,128]{1,0:T(8,128)(2,1)S(1)} %copy-done.3, ...), custom_call_target="tpu_custom_call" | custom-call | tf_op jit(solution)/shard_map/graph_layer/pallas_call | solution.py:516
  121.8 0.6 copy.18
  122.4 0.6 copy.19
  123.0 0.6 copy.20
  (7 shorter events, 0.0 us)
Async XLA Ops:
  4.2 2.2 %copy-start = (bf16[1,1,2,32,2,128,128]{6,5,4,3,2,1,0:T(8,128)(2,1)S(1)}, bf16[1,1,2,32,2,128,128]{6,5,4,3,2,1,0:T(8,128)(2,1)}, u32[]{:S(2)}) copy-start(bf16[1,1,2,32,2,128,128]{6,5,4,3,2,1,0:T(8,128)(2,1)} %param.8) | copy-start | bytes 12582916
  6.4 0.8 copy-start.1
  7.1 0.8 copy-start.2
  7.9 0.8 copy-start.3

commit v3 on v2

--- a/solution.py
+++ b/solution.py
@@ -18,15 +18,22 @@
 
 
 def kernel(
-    table,
-    feat,
-    weight,
-    up,
+    feat_hbm,
+    weight_hbm,
+    up_hbm,
     adj_hbm,
+    rows_hbm,
+    live_hbm,
     hidden,
     input_grad,
     weight_grad,
     adj,
+    up,
+    weight,
+    rows_v,
+    live_v,
+    tab_v,
+    table,
     feats,
     sums,
     c1_out,
@@ -50,7 +57,7 @@
     h2_buf,
     h3_buf,
     wg_all,
-    adj_sem,
+    in_sem,
     az_s,
     az_r,
     ax_s,
@@ -116,8 +123,21 @@
             src_ref=src, dst_ref=dst, send_sem=ss, recv_sem=rs, device_id=dev, device_id_type=MESH
         )
 
-    load = pltpu.make_async_copy(adj_hbm, adj, adj_sem)
-    load.start()
+    in_copies = [
+        pltpu.make_async_copy(src, dst, in_sem.at[i])
+        for i, (src, dst) in enumerate(
+            (
+                (feat_hbm, feats.at[b]),
+                (rows_hbm, rows_v),
+                (live_hbm, live_v),
+                (weight_hbm, weight),
+                (adj_hbm, adj),
+                (up_hbm, up),
+            )
+        )
+    ]
+    for copy in in_copies:
+        copy.start()
 
     bar = pltpu.get_barrier_semaphore()
 
@@ -132,7 +152,58 @@
         greet(at_y(d))
     for dev in (sib, (b_up, r), (b_dn, r), (b_up, r_oz), (b_dn, r_oz)):
         greet(dev)
-    pl.semaphore_wait(bar, (ZH * ZL - 1) + (X - 1) + (Y - 1) + 5)
+
+    half, zq = z // ZQ, z % ZQ
+    ohalf = 1 - half
+
+    in_copies[1].wait()
+    in_copies[2].wait()
+    i_s = lax.broadcasted_iota(jnp.int32, (BLK, BLK), 0)
+    i_l = lax.broadcasted_iota(jnp.int32, (BLK, BLK), 1)
+
+    def rank(n):
+        far = ((n // ZQ) % 2) ^ half
+        return (far * ZQ + ((zq - n % ZQ) & (ZQ - 1))) * X + ((x - n // ZL) & (X - 1))
+
+    rank_s, rank_l = rank(i_s), rank(i_l)
+
+    def to_rows(lanes):
+        return jnp.sum(jnp.where(i_s == i_l, lanes, 0), axis=1, keepdims=True)
+
+    t_l = lax.broadcasted_iota(jnp.int32, (BLK, REP), 1)
+    for s in range(2):
+        row_s = [to_rows(rows_v[s, k : k + 1, :]) for k in range(2)]
+        live_l = live_v[s : s + 1, :]
+        live_s = to_rows(live_l)
+        code = [(2 * rank_s + k) * 1024 + s * SL + 2 * i_s + k for k in range(2)]
+
+        def best(hits):
+            found = jnp.max(jnp.maximum(hits[0], hits[1]), axis=0, keepdims=True)
+            return jnp.where(found < 0, 2 * SL, found & 1023)
+
+        for k in range(2):
+            row_l = rows_v[s, k : k + 1, :]
+            hits = [
+                jnp.where(
+                    (row_s[o] == row_l) & (live_s > o) & (2 * rank_s + o < 2 * rank_l + k),
+                    code[o],
+                    -1,
+                )
+                for o in range(2)
+            ]
+            tab_v[2 * s + k : 2 * s + k + 1, :BLK] = best(hits)
+            spot = ((((row_l & 1) * Y + ((row_l // 2) & (Y - 1))) * 2 + s) * ZH) + row_l // (2 * Y)
+            tab_v[6 + 2 * s + k : 7 + 2 * s + k, :BLK] = jnp.where(live_l > k, spot, 2 * REP)
+        hits = [
+            jnp.where((row_s[o] == t_l) & (live_s > o), code[o][:, :1], -1) for o in range(2)
+        ]
+        tab_v[4 + s : 5 + s, :REP] = best(hits)
+    to_scalars = pltpu.make_async_copy(tab_v, table, in_sem.at[6])
+    to_scalars.start()
+    sums[2 * SL] = jnp.zeros((T, T), f32)
+    slopes[2 * REP] = jnp.zeros((T, T), bf16)
+    in_copies[0].wait()
+    in_copies[3].wait()
 
     sends = []
 
@@ -141,76 +212,127 @@
         sends.append(copy)
         return copy
 
-    for d in range(1, ZL):
-        go(rc(feat, feats.at[b], az_s.at[d], az_r.at[d], at_z(d)))
-    for e in range(1, X):
-        go(rc(feat, feats.at[b], ax_s.at[e, 0], ax_r.at[e, 0], at_x(e)))
-    feats[b] = feat[...]
-    sums[2 * SL] = jnp.zeros((T, T), f32)
-    slopes[2 * REP] = jnp.zeros((T, T), bf16)
-    for d in range(1, ZL):
-        n = x * ZL + (z + ZL - d) % ZL
-        rc(feat, feats.at[n], az_s.at[d], az_r.at[d], at_z(d)).wait_recv()
+    pl.semaphore_wait(bar, (ZH * ZL - 1) + (X - 1) + (Y - 1) + 5)
+
+    def zsrc(g):
+        return (half, ohalf)[g // ZQ] * ZQ + (zq + ZQ - g % ZQ) % ZQ
+
+    def mate(m):
+        return (x * ZL + half * ZQ + (zq + m) % ZQ, r)
+
+    partner = (x * ZL + ohalf * ZQ + zq, r)
+
+    def az_copy(g, v, dev):
+        slot = feats.at[x * ZL + v]
+        return rc(slot, slot, az_s.at[g], az_r.at[g], dev)
+
+    def ax_copy(g, e, v):
+        slot = feats.at[v * ZL + zsrc(g)]
+        return rc(slot, slot, ax_s.at[e, g], ax_r.at[e, g], at_x(e))
+
+    def along_x(g):
         for e in range(1, X):
-            go(rc(feats.at[n], feats.at[n], ax_s.at[e, d], ax_r.at[e, d], at_x(e)))
-    for d in range(0, ZL):
-        for e in range(1, X):
-            n = ((x + X - e) % X) * ZL + (z + ZL - d) % ZL
-            rc(feat, feats.at[n], ax_s.at[e, d], ax_r.at[e, d], at_x(e)).wait_recv()
-    load.wait()
+            go(ax_copy(g, e, x))
+
+    go(az_copy(ZQ, z, partner))
+    for m in range(1, ZQ):
+        go(az_copy(m, z, mate(m)))
+    along_x(0)
+    for m in range(1, ZQ):
+        az_copy(m, zsrc(m), mate(m)).wait_recv()
+        along_x(m)
+    az_copy(ZQ, zsrc(ZQ), partner).wait_recv()
+    for m in range(1, ZQ):
+        go(az_copy(ZQ + m, zsrc(ZQ), mate(m)))
+    along_x(ZQ)
+    in_copies[4].wait()
+    to_scalars.wait()
 
     w = weight[...]
 
-    def forward(n, carry):
-        mixed = dot(feats[n], w).astype(bf16)
-        for s in range(2):
-            q = s * SL + 2 * n
-            a = adj[pl.ds(q, 2)].reshape(2 * T, T)
-            prod = dot(a, mixed)
-            sums[q] = prod[:T] + sums[table[q]]
-            sums[q + 1] = prod[T:] + sums[table[q + 1]]
-        return carry
-
-    lax.fori_loop(0, BLK, forward, 0)
+    def forward(g):
+        for e in range(X):
+            v = (x + X - e) % X
+            if e:
+                ax_copy(g, e, v).wait_recv()
+            n = v * ZL + zsrc(g)
+            mixed = dot(feats[n], w).astype(bf16)
+            for s in range(2):
+                q = s * SL + 2 * n
+                prod = dot(adj[pl.ds(q, 2)].reshape(2 * T, T), mixed)
+                sums[q] = prod[:T] + sums[table[2 * s, n]]
+                sums[q + 1] = prod[T:] + sums[table[2 * s + 1, n]]
+
+    early = ZQ - 1
+    for g in range(early):
+        forward(g)
+    for m in range(1, ZQ):
+        az_copy(ZQ + m, zsrc(ZQ + m), mate(m)).wait_recv()
+        along_x(ZQ + m)
+    for g in range(early, ZL):
+        forward(g)
 
     def routed(s, t):
-        return sums[table[2 * SL + s * REP + t]]
+        return sums[table[4 + s, t]]
 
     order = tuple(range(1, Y)) + (0,)
-    for d in order:
-        yy = (y + d) % Y
-        for s in range(2):
-            for h in range(ZH):
-                c1_out[d, s * ZH + h] = routed(s, rep_of(h, yy, 1 - core)).astype(bf16)
-        go(rc(c1_out.at[d], c1_in.at[d], c1_s.at[d], c1_r.at[d], sib))
-    for d in order:
-        yy = (y + d) % Y
-        rc(c1_out.at[d], c1_in.at[d], c1_s.at[d], c1_r.at[d], sib).wait_recv()
-        for s in range(2):
-            for h in range(ZH):
-                both = routed(s, rep_of(h, yy, core)) + c1_in[d, s * ZH + h].astype(f32)
+    sides = (ozh, zh)
+
+    def c1_copy(k, d):
+        return rc(c1_out.at[k, d], c1_in.at[k, d], c1_s.at[k, d], c1_r.at[k, d], sib)
+
+    def c2_copy(k, d):
+        return rc(c2_out.at[k, d], c2_in.at[k, d], c2_s.at[k, d], c2_r.at[k, d], at_y(d))
+
+    for k in range(2):
+        for d in order:
+            for s in range(2):
+                c1_out[k, d, s] = routed(s, rep_of(sides[k], (y + d) % Y, 1 - core)).astype(bf16)
+            go(c1_copy(k, d))
+    for k in range(2):
+        for d in order:
+            c1_copy(k, d).wait_recv()
+            for s in range(2):
+                both = routed(s, rep_of(sides[k], (y + d) % Y, core)) + c1_in[k, d, s].astype(f32)
                 if d:
-                    c2_out[d, s * ZH + h] = both.astype(bf16)
+                    c2_out[k, d, s] = both.astype(bf16)
                 else:
-                    part[s * ZH + h] = both
-        if d:
-            go(rc(c2_out.at[d], c2_in.at[d], c2_s.at[d], c2_r.at[d], at_y(d)))
-    for d in range(1, Y):
-        rc(c2_out.at[d], c2_in.at[d], c2_s.at[d], c2_r.at[d], at_y(d)).wait_recv()
-    for i in range(2 * ZH):
-        total = part[i]
+                    part[k, s] = both
+            if d:
+                go(c2_copy(k, d))
+
+    first, last = (ZL - z) // ZL, (z + 1) // ZL
+
+    def c3_copy(i):
+        dev = (
+            (b, r_oz),
+            (b_dn, r),
+            (b_dn, rep_of((zh + first) % ZH, y, core)),
+        )[i]
+        return rc(c3_out.at[i], c3_in.at[i], c3_s.at[i], c3_r.at[i], dev)
+
+    def reduced(k, s):
+        t = part[k, s]
         for d in range(1, Y):
-            total = total + c2_in[d, i].astype(f32)
-        part[i] = total
-    c3_to = ((b, r_oz), (b_dn, r_oz), (b_dn, r))
-    for i, pick in enumerate((ozh, ZH + ozh, ZH + zh)):
-        c3_out[i] = part[pick].astype(bf16)
-        go(rc(c3_out.at[i], c3_in.at[i], c3_s.at[i], c3_r.at[i], c3_to[i]))
-    summed = part[zh]
-    for i in range(3):
-        rc(c3_out.at[i], c3_in.at[i], c3_s.at[i], c3_r.at[i], c3_to[i]).wait_recv()
-        summed = summed + c3_in[i].astype(f32)
-
+            t = t + c2_in[k, d, s].astype(f32)
+        return t
+
+    for k in range(2):
+        for d in range(1, Y):
+            c2_copy(k, d).wait_recv()
+        c3_out[2 - k] = reduced(k, 1).astype(bf16)
+        go(c3_copy(2 - k))
+    c3_copy(2).wait_recv()
+    near = c3_in[2].astype(f32)
+    c3_out[0] = (reduced(0, 0) + jnp.where(last == 0, near, 0.0)).astype(bf16)
+    go(c3_copy(0))
+    summed = reduced(1, 0) + jnp.where(last == 0, 0.0, near)
+    c3_copy(1).wait_recv()
+    summed = summed + c3_in[1].astype(f32)
+    c3_copy(0).wait_recv()
+    summed = summed + c3_in[0].astype(f32)
+
+    in_copies[5].wait()
     sig = jax.nn.sigmoid(summed)
     slope = up[...].astype(f32) * (sig * (1.0 + summed * (1.0 - sig)))
 
@@ -224,11 +346,20 @@
 
     slopes[place(0, zh, y, core)] = slope.T.astype(bf16)
     own, helps = tile(0, y, core), tile(1, y, core)
-    e1 = ((own, (b, r_oz)), (helps, (b_up, r_oz)), (helps, (b_up, r)))
+    turn = (ozh + last) % ZH
+    e1 = (
+        (own, own, (b, r_oz)),
+        (own, helps, (b_up, r)),
+        (
+            slopes.at[place(0, turn, y, core)],
+            slopes.at[place(1, turn, y, core)],
+            (b_up, rep_of((zh + last) % ZH, y, core)),
+        ),
+    )
 
     def e1_copy(i):
-        dst, dev = e1[i]
-        return rc(own, dst, e1_s.at[i], e1_r.at[i], dev)
+        src, dst, dev = e1[i]
+        return rc(src, dst, e1_s.at[i], e1_r.at[i], dev)
 
     def e2_copy(j, d, v):
         return rc(tile(j, v, core), tile(j, v, core), e2_s.at[j, d], e2_r.at[j, d], at_y(d))
@@ -247,33 +378,31 @@
             e2_copy(j, d, (y + Y - d) % Y).wait_recv()
             go(e3_copy(j, d, core))
 
-    for i in range(3):
-        go(e1_copy(i))
+    go(e1_copy(0))
+    go(e1_copy(1))
     spread(0)
     hidden[...] = (summed * sig).astype(bf16)
-    e1_copy(2).wait_recv()
+    e1_copy(1).wait_recv()
     spread(1)
     pass_on(0)
     e1_copy(0).wait_recv()
+    go(e1_copy(2))
     spread(2)
-    e1_copy(1).wait_recv()
+    pass_on(1)
+    e1_copy(2).wait_recv()
     spread(3)
-    for j in range(1, 4):
+    for j in range(2, 4):
         pass_on(j)
     for j in range(4):
         for d in range(Y):
             e3_copy(j, d, 1 - core).wait_recv()
-
-    base = 2 * SL + 2 * REP
-    half, zq = z // ZQ, z % ZQ
-    ohalf = 1 - half
 
     def backward(n):
         out = None
         for s in range(2):
             q = s * SL + 2 * n
             lhs = jnp.concatenate(
-                [slopes[table[base + q]], slopes[table[base + q + 1]]], axis=1
+                [slopes[table[6 + 2 * s, n]], slopes[table[7 + 2 * s, n]]], axis=1
             )
             term = dot(lhs, adj[pl.ds(q, 2)].reshape(2 * T, T))
             out = term if out is None else out + term
@@ -413,38 +542,12 @@
         copy.wait_send()
 
 
-def tables(row_tiles, live_counts, blocks, reps):
-    slots = 2 * blocks
-    row = row_tiles.reshape(2, slots)
-    count = jnp.repeat(live_counts.reshape(2, blocks), 2, axis=1)
-    q = jnp.arange(slots, dtype=jnp.int32)
-    alive = (q % 2)[None] < count
-    key = jnp.where(alive, row, reps)
-    want = jnp.concatenate(
-        [key, jnp.broadcast_to(jnp.arange(reps, dtype=jnp.int32), (2, reps))], axis=1
-    )
-    limit = jnp.concatenate([q, jnp.full((reps,), slots, jnp.int32)])
-    hit = (
-        (key[:, None, :] == want[:, :, None])
-        & alive[:, None, :]
-        & (q[None, None, :] < limit[None, :, None])
-    )
-    at = q[None] + slots * jnp.arange(2, dtype=jnp.int32)[:, None]
-    found = jnp.max(jnp.where(hit, at[:, None, :], -1), axis=2)
-    found = jnp.where(found < 0, 2 * slots, found)
-    h, v, c = row // (2 * Y), (row // 2) % Y, row % 2
-    s = jnp.arange(2, dtype=jnp.int32)[:, None]
-    pos = jnp.where(alive, ((c * Y + v) * 2 + s) * ZH + h, 2 * reps)
-    return jnp.concatenate(
-        [found[:, :slots].reshape(-1), found[:, slots:].reshape(-1), pos.reshape(-1)]
-    )
-
-
 def local(features, weight, adjacency, row_tiles, live_counts, upstream):
     BLK, REP = X * ZL, ZH * Y * 2
     f32, bf16 = jnp.float32, jnp.bfloat16
-    table = tables(row_tiles, live_counts, BLK, REP)
     adj = adjacency.reshape(4 * BLK, T, T)
+    rows = jnp.swapaxes(row_tiles, 3, 4).reshape(2, 2, BLK)
+    live = live_counts.reshape(2, BLK)
     vmem = pl.BlockSpec(memory_space=pltpu.VMEM)
 
     def buf(*dims, dtype=bf16):
@@ -454,13 +557,19 @@
     dma = pltpu.SemaphoreType.DMA
     scratch = [
         buf(4 * BLK, T),
+        buf(T),
+        buf(T),
+        pltpu.VMEM((2, 2, BLK), jnp.int32),
+        pltpu.VMEM((2, BLK), jnp.int32),
+        buf(16, dtype=jnp.int32),
+        pltpu.SMEM((16, T), jnp.int32),
         buf(BLK, T),
         buf(4 * BLK + 1, T, dtype=f32),
-        buf(Y, 2 * ZH, T),
-        buf(Y, 2 * ZH, T),
-        buf(Y, 2 * ZH, T),
-        buf(Y, 2 * ZH, T),
-        buf(2 * ZH, T, dtype=f32),
+        buf(2, Y, 2, T),
+        buf(2, Y, 2, T),
+        buf(2, Y, 2, T),
+        buf(2, Y, 2, T),
+        buf(2, 2, T, dtype=f32),
         buf(3, T),
         buf(3, T),
         buf(2 * REP + 1, T),
@@ -477,15 +586,15 @@
         buf(ZH * ZL, U),
         buf(X, U, dtype=f32),
         buf(2 * Y, U, dtype=f32),
-        dma,
+        dma((7,)),
         dma((ZL,)),
         dma((ZL,)),
         dma((X, ZL)),
         dma((X, ZL)),
-        dma((Y,)),
-        dma((Y,)),
-        dma((Y,)),
-        dma((Y,)),
+        dma((2, Y)),
+        dma((2, Y)),
+        dma((2, Y)),
+        dma((2, Y)),
         dma((3,)),
         dma((3,)),
         dma((3,)),
@@ -521,19 +630,13 @@
             jax.ShapeDtypeStruct((T, T), bf16),
             jax.ShapeDtypeStruct((T, T), f32),
         ),
-        in_specs=[
-            pl.BlockSpec(memory_space=pltpu.SMEM),
-            vmem,
-            vmem,
-            vmem,
-            pl.BlockSpec(memory_space=pl.ANY),
-        ],
+        in_specs=[pl.BlockSpec(memory_space=pltpu.HBM)] * 6,
         out_specs=(vmem, vmem, vmem),
         scratch_shapes=scratch,
         compiler_params=pltpu.CompilerParams(
-            collective_id=0, has_side_effects=True, vmem_limit_bytes=48 * 1024 * 1024
+            collective_id=0, has_side_effects=True, vmem_limit_bytes=64 * 1024 * 1024
         ),
-    )(table, features, weight, upstream, adj)
+    )(features, weight, upstream, adj, rows, live)
 
 
 def solution(mesh):

time: 124 us -> 106 us (0.85)
  Pallas kernels: 113 us -> 101 us
  local copies, waits for them, and re-layouts: 8.75 us -> 4.22 us
    pallas_call x1, Pallas kernels: 113 us -> 101 us  [local(): pl.pallas_call(kernel, name='graph_layer', out_shape=(jax.ShapeDtypeStruc...]
    unnamed x12 -> x3, local copies, waits for them, and re-layouts: 7.09 us -> 4.22 us
where the time goes in v3:
time: 106 us
  Pallas kernels  101 us (95%)
  local copies, waits for them, and re-layouts  4.22 us (4%)
    pallas_call x1, Pallas kernels, local(): pl.pallas_call(kernel, name='graph_layer', out_shape=(jax.ShapeDtypeStruc...  101 us
    unnamed x3, local copies, waits for them, and re-layouts  4.22 us

profile of v3, /device:TPU:1, one launch (start us, length us, event | category | flops | bytes accessed | tf_op | source)
XLA Modules:
  0.0 105.8 jit_solution(2215751440749684110)
XLA Ops:
  0.6 100.9 %graph_layer.1 = (bf16[128,128]{1,0:T(8,128)(2,1)}, bf16[128,128]{1,0:T(8,128)(2,1)}, f32[128,128]{1,0:T(8,128)}) custom-call(bf16[128,128]{1,0:T(8,128)(2,1)} %feat_hbm.1, bf16[128,128]{1,0:T(8,128)(2,1)} %weight_hbm.1, bf16[128,128]{1,0:T(8,128)(2,1)} %up_hbm.1, bf16[128,128,128]{2,1,0:T(8,128)(2,1)} %bitcast.5, s32[2,2,32]{2,1,0:T(2,128)} %bitcast.6, ...), custom_call_target="tpu_custom_call" | custom-call | tf_op jit(solution)/shard_map/graph_layer/pallas_call | solution.py:625
  101.6 1.4 %copy.12 = bf16[128,128]{1,0:T(8,128)(2,1)} copy(bf16[128,128]{1,0:T(8,128)(2,1)} %get-tuple-element.6) | data formatting | bytes 65536
  102.9 1.4 %copy.13 = bf16[128,128]{1,0:T(8,128)(2,1)} copy(bf16[128,128]{1,0:T(8,128)(2,1)} %get-tuple-element.7) | data formatting | bytes 65536
  104.3 1.5 %copy.14 = f32[128,128]{1,0:T(8,128)} copy(f32[128,128]{1,0:T(8,128)} %get-tuple-element.8) | data formatting | bytes 131072

commit v4 on v3

--- a/solution.py
+++ b/solution.py
@@ -29,6 +29,7 @@
     weight_grad,
     adj,
     up,
+    up_far,
     weight,
     rows_v,
     live_v,
@@ -62,14 +63,14 @@
     az_r,
     ax_s,
     ax_r,
+    up_s,
+    up_r,
     c1_s,
     c1_r,
     c2_s,
     c2_r,
     c3_s,
     c3_r,
-    e1_s,
-    e1_r,
     e2_s,
     e2_r,
     e3_s,
@@ -115,6 +116,14 @@
     def at_y(d):
         return (b, rep_of(zh, (y + d) % Y, core))
 
+    first, last = (ZL - z) // ZL, (z + 1) // ZL
+
+    def at_dn(d):
+        return (b_dn, rep_of((zh + first) % ZH, (y + d) % Y, core))
+
+    def at_up(d):
+        return (b_up, rep_of((zh + last) % ZH, (y + d) % Y, core))
+
     sib = (b, rep_of(zh, y, 1 - core))
     r_oz = rep_of(ozh, y, core)
 
@@ -150,8 +159,10 @@
         greet(at_x(d))
     for d in range(1, Y):
         greet(at_y(d))
-    for dev in (sib, (b_up, r), (b_dn, r), (b_up, r_oz), (b_dn, r_oz)):
-        greet(dev)
+    greet(sib)
+    for d in range(Y):
+        greet(at_up(d))
+        greet(at_dn(d))
 
     half, zq = z // ZQ, z % ZQ
     ohalf = 1 - half
@@ -212,7 +223,7 @@
         sends.append(copy)
         return copy
 
-    pl.semaphore_wait(bar, (ZH * ZL - 1) + (X - 1) + (Y - 1) + 5)
+    pl.semaphore_wait(bar, (ZH * ZL - 1) + (X - 1) + (Y - 1) + 1 + 2 * Y)
 
     def zsrc(g):
         return (half, ohalf)[g // ZQ] * ZQ + (zq + ZQ - g % ZQ) % ZQ
@@ -275,127 +286,92 @@
     def routed(s, t):
         return sums[table[4 + s, t]]
 
+    def up_copy():
+        return rc(up, up_far, up_s, up_r, (b, r_oz))
+
+    in_copies[5].wait()
+    go(up_copy())
     order = tuple(range(1, Y)) + (0,)
-    sides = (ozh, zh)
-
-    def c1_copy(k, d):
-        return rc(c1_out.at[k, d], c1_in.at[k, d], c1_s.at[k, d], c1_r.at[k, d], sib)
-
-    def c2_copy(k, d):
-        return rc(c2_out.at[k, d], c2_in.at[k, d], c2_s.at[k, d], c2_r.at[k, d], at_y(d))
-
-    for k in range(2):
-        for d in order:
-            for s in range(2):
-                c1_out[k, d, s] = routed(s, rep_of(sides[k], (y + d) % Y, 1 - core)).astype(bf16)
-            go(c1_copy(k, d))
-    for k in range(2):
-        for d in order:
-            c1_copy(k, d).wait_recv()
-            for s in range(2):
-                both = routed(s, rep_of(sides[k], (y + d) % Y, core)) + c1_in[k, d, s].astype(f32)
-                if d:
-                    c2_out[k, d, s] = both.astype(bf16)
+
+    def c1_copy(d):
+        return rc(c1_out.at[d], c1_in.at[d], c1_s.at[d], c1_r.at[d], sib)
+
+    def c2_copy(s, d):
+        dev = at_dn(d) if s else at_y(d)
+        return rc(c2_out.at[s, d], c2_in.at[s, d], c2_s.at[s, d], c2_r.at[s, d], dev)
+
+    for d in order:
+        for s in range(2):
+            for h in range(ZH):
+                c1_out[d, s, h] = routed(s, rep_of(h, (y + d) % Y, 1 - core)).astype(bf16)
+        go(c1_copy(d))
+    for d in order:
+        c1_copy(d).wait_recv()
+        for s in (1, 0):
+            for h in range(ZH):
+                both = routed(s, rep_of(h, (y + d) % Y, core)) + c1_in[d, s, h].astype(f32)
+                if s or d:
+                    c2_out[s, d, h] = both.astype(bf16)
                 else:
-                    part[k, s] = both
-            if d:
-                go(c2_copy(k, d))
-
-    first, last = (ZL - z) // ZL, (z + 1) // ZL
-
-    def c3_copy(i):
-        dev = (
-            (b, r_oz),
-            (b_dn, r),
-            (b_dn, rep_of((zh + first) % ZH, y, core)),
-        )[i]
-        return rc(c3_out.at[i], c3_in.at[i], c3_s.at[i], c3_r.at[i], dev)
-
-    def reduced(k, s):
-        t = part[k, s]
-        for d in range(1, Y):
-            t = t + c2_in[k, d, s].astype(f32)
-        return t
-
-    for k in range(2):
-        for d in range(1, Y):
-            c2_copy(k, d).wait_recv()
-        c3_out[2 - k] = reduced(k, 1).astype(bf16)
-        go(c3_copy(2 - k))
-    c3_copy(2).wait_recv()
-    near = c3_in[2].astype(f32)
-    c3_out[0] = (reduced(0, 0) + jnp.where(last == 0, near, 0.0)).astype(bf16)
-    go(c3_copy(0))
-    summed = reduced(1, 0) + jnp.where(last == 0, 0.0, near)
-    c3_copy(1).wait_recv()
-    summed = summed + c3_in[1].astype(f32)
-    c3_copy(0).wait_recv()
-    summed = summed + c3_in[0].astype(f32)
-
-    in_copies[5].wait()
-    sig = jax.nn.sigmoid(summed)
-    slope = up[...].astype(f32) * (sig * (1.0 + summed * (1.0 - sig)))
+                    part[h] = both
+            if s or d:
+                go(c2_copy(s, d))
+
+    for s in range(2):
+        for d in range(1 - s, Y):
+            c2_copy(s, d).wait_recv()
+    for h in range(ZH):
+        t = part[h]
+        for s in range(2):
+            for d in range(1 - s, Y):
+                t = t + c2_in[s, d, h].astype(f32)
+        part[h] = t
+        c3_out[h] = t.astype(bf16)
+
+    def c3_copy():
+        return rc(c3_out, c3_in, c3_s, c3_r, (b, r_oz))
+
+    go(c3_copy())
+    up_copy().wait_recv()
+    c3_copy().wait_recv()
 
     def place(s, h, v, c):
         return ((c * Y + v) * 2 + s) * ZH + h
 
-    kinds = ((0, zh), (1, zh), (0, ozh), (1, ozh))
-
-    def tile(j, v, c):
-        return slopes.at[place(*kinds[j], v, c)]
-
-    slopes[place(0, zh, y, core)] = slope.T.astype(bf16)
-    own, helps = tile(0, y, core), tile(1, y, core)
-    turn = (ozh + last) % ZH
-    e1 = (
-        (own, own, (b, r_oz)),
-        (own, helps, (b_up, r)),
-        (
-            slopes.at[place(0, turn, y, core)],
-            slopes.at[place(1, turn, y, core)],
-            (b_up, rep_of((zh + last) % ZH, y, core)),
-        ),
-    )
-
-    def e1_copy(i):
-        src, dst, dev = e1[i]
-        return rc(src, dst, e1_s.at[i], e1_r.at[i], dev)
-
-    def e2_copy(j, d, v):
-        return rc(tile(j, v, core), tile(j, v, core), e2_s.at[j, d], e2_r.at[j, d], at_y(d))
-
-    def e3_copy(j, d, c):
-        got = tile(j, (y + Y - d) % Y, c)
-        return rc(got, got, e3_s.at[j, d], e3_r.at[j, d], sib)
-
-    def spread(j):
-        for d in range(1, Y):
-            go(e2_copy(j, d, y))
-        go(e3_copy(j, 0, core))
-
-    def pass_on(j):
-        for d in range(1, Y):
-            e2_copy(j, d, (y + Y - d) % Y).wait_recv()
-            go(e3_copy(j, d, core))
-
-    go(e1_copy(0))
-    go(e1_copy(1))
-    spread(0)
-    hidden[...] = (summed * sig).astype(bf16)
-    e1_copy(1).wait_recv()
-    spread(1)
-    pass_on(0)
-    e1_copy(0).wait_recv()
-    go(e1_copy(2))
-    spread(2)
-    pass_on(1)
-    e1_copy(2).wait_recv()
-    spread(3)
-    for j in range(2, 4):
-        pass_on(j)
-    for j in range(4):
+    for h in range(ZH):
+        summed = part[h] + c3_in[h].astype(f32)
+        sig = jax.nn.sigmoid(summed)
+        given = jnp.where(zh == h, up[...], up_far[...]).astype(f32)
+        slope = given * (sig * (1.0 + summed * (1.0 - sig)))
+        slopes[place(0, h, y, core)] = slope.T.astype(bf16)
+        part[h] = summed * sig
+
+    def pair(s, v, c):
+        return slopes.at[pl.ds(place(s, 0, v, c), ZH)]
+
+    def e2_copy(s, d):
+        dev = at_up(d) if s else at_y(d)
+        own = pair(0, y, core)
+        return rc(own, pair(s, y, core), e2_s.at[s, d], e2_r.at[s, d], dev)
+
+    def e3_copy(s, d, c):
+        got = pair(s, (y + Y - d) % Y, c)
+        return rc(got, got, e3_s.at[s, d], e3_r.at[s, d], sib)
+
+    for d in order:
+        go(e2_copy(1, d))
+        if d:
+            go(e2_copy(0, d))
+    go(e3_copy(0, 0, core))
+    hidden[...] = part[zh].astype(bf16)
+    for d in (0,) + order[:-1]:
+        for s in range(2):
+            if s or d:
+                e2_copy(s, d).wait_recv()
+                go(e3_copy(s, d, core))
+    for s in range(2):
         for d in range(Y):
-            e3_copy(j, d, 1 - core).wait_recv()
+            e3_copy(s, d, 1 - core).wait_recv()
 
     def backward(n):
         out = None
@@ -559,19 +535,20 @@
         buf(4 * BLK, T),
         buf(T),
         buf(T),
+        buf(T),
         pltpu.VMEM((2, 2, BLK), jnp.int32),
         pltpu.VMEM((2, BLK), jnp.int32),
         buf(16, dtype=jnp.int32),
         pltpu.SMEM((16, T), jnp.int32),
         buf(BLK, T),
         buf(4 * BLK + 1, T, dtype=f32),
-        buf(2, Y, 2, T),
-        buf(2, Y, 2, T),
-        buf(2, Y, 2, T),
-        buf(2, Y, 2, T),
-        buf(2, 2, T, dtype=f32),
-        buf(3, T),
-        buf(3, T),
+        buf(Y, 2, ZH, T),
+        buf(Y, 2, ZH, T),
+        buf(2, Y, ZH, T),
+        buf(2, Y, ZH, T),
+        buf(ZH, T, dtype=f32),
+        buf(ZH, T),
+        buf(ZH, T),
         buf(2 * REP + 1, T),
         buf(BLK, T),
         buf(2, X, ZQ, T),
@@ -591,18 +568,18 @@
         dma((ZL,)),
         dma((X, ZL)),
         dma((X, ZL)),
+        dma,
+        dma,
+        dma((Y,)),
+        dma((Y,)),
+        dma((2, Y)),
+        dma((2, Y)),
+        dma,
+        dma,
         dma((2, Y)),
         dma((2, Y)),
         dma((2, Y)),
         dma((2, Y)),
-        dma((3,)),
-        dma((3,)),
-        dma((3,)),
-        dma((3,)),
-        dma((4, Y)),
-        dma((4, Y)),
-        dma((4, Y)),
-        dma((4, Y)),
         dma((2, X)),
         dma((2, X)),
         dma((2, ZQ)),
@@ -634,9 +611,14 @@
         out_specs=(vmem, vmem, vmem),
         scratch_shapes=scratch,
         compiler_params=pltpu.CompilerParams(
-            collective_id=0, has_side_effects=True, vmem_limit_bytes=64 * 1024 * 1024
+            collective_id=0, has_side_effects=True, vmem_limit_bytes=48 * 1024 * 1024
         ),
-    )(features, weight, upstream, adj, rows, live)
+    )(
+        *(
+            pltpu.with_memory_space_constraint(v, pltpu.HBM)
+            for v in (features, weight, upstream, adj, rows, live)
+        )
+    )
 
 
 def solution(mesh):

time: 106 us -> 101 us (0.953)
  Pallas kernels: 101 us -> 98.6 us
  local copies, waits for them, and re-layouts: 4.22 us -> 1.86 us
    unnamed x3, local copies, waits for them, and re-layouts: 4.22 us -> 1.86 us
    pallas_call x1, Pallas kernels: 101 us -> 98.6 us  [local(): pl.pallas_call(kernel, name='graph_layer', out_shape=(jax.ShapeDtypeStruc...]
where the time goes in v4:
time: 101 us
  Pallas kernels  98.6 us (98%)
  local copies, waits for them, and re-layouts  1.86 us (2%)
    pallas_call x1, Pallas kernels, local(): pl.pallas_call(kernel, name='graph_layer', out_shape=(jax.ShapeDtypeStruc...  98.6 us

profile of v4, /device:TPU:1, one launch (start us, length us, event | category | flops | bytes accessed | tf_op | source)
XLA Modules:
  0.0 101.1 jit_solution(2852031004726313494)
XLA Ops:
  0.6 98.6 %graph_layer.1 = (bf16[128,128]{1,0:T(8,128)(2,1)S(1)}, bf16[128,128]{1,0:T(8,128)(2,1)S(1)}, f32[128,128]{1,0:T(8,128)S(1)}) custom-call(bf16[128,128]{1,0:T(8,128)(2,1)} %feat_hbm.1, bf16[128,128]{1,0:T(8,128)(2,1)} %weight_hbm.1, bf16[128,128]{1,0:T(8,128)(2,1)} %up_hbm.1, bf16[128,128,128]{2,1,0:T(8,128)(2,1)} %bitcast.5, s32[2,2,32]{2,1,0:T(2,128)} %bitcast.6, ...), custom_call_target="tpu_custom_call" | custom-call | tf_op jit(solution)/shard_map/graph_layer/pallas_call | solution.py:602
  99.3 0.6 copy.12
  99.9 0.6 copy.13
  100.5 0.6 copy.14

commit v5 on v4

--- a/solution.py
+++ b/solution.py
@@ -44,6 +44,7 @@
     part,
     c3_out,
     c3_in,
+    tops,
     slopes,
     terms,
     gx_in,
@@ -223,6 +224,12 @@
         sends.append(copy)
         return copy
 
+    def flush(keep):
+        done = sends[: len(sends) - keep]
+        del sends[: len(done)]
+        for copy in done:
+            copy.wait_send()
+
     pl.semaphore_wait(bar, (ZH * ZL - 1) + (X - 1) + (Y - 1) + 1 + 2 * Y)
 
     def zsrc(g):
@@ -259,7 +266,6 @@
     in_copies[4].wait()
     to_scalars.wait()
 
-    w = weight[...]
 
     def forward(g):
         for e in range(X):
@@ -267,10 +273,9 @@
             if e:
                 ax_copy(g, e, v).wait_recv()
             n = v * ZL + zsrc(g)
-            mixed = dot(feats[n], w).astype(bf16)
             for s in range(2):
                 q = s * SL + 2 * n
-                prod = dot(adj[pl.ds(q, 2)].reshape(2 * T, T), mixed)
+                prod = dot(adj[pl.ds(q, 2)].reshape(2 * T, T), feats[n])
                 sums[q] = prod[:T] + sums[table[2 * s, n]]
                 sums[q + 1] = prod[T:] + sums[table[2 * s + 1, n]]
 
@@ -293,85 +298,125 @@
     go(up_copy())
     order = tuple(range(1, Y)) + (0,)
 
-    def c1_copy(d):
-        return rc(c1_out.at[d], c1_in.at[d], c1_s.at[d], c1_r.at[d], sib)
-
-    def c2_copy(s, d):
+    def c1_copy(h, d):
+        return rc(c1_out.at[h, d], c1_in.at[h, d], c1_s.at[h, d], c1_r.at[h, d], sib)
+
+    def c2_copy(h, s, d):
         dev = at_dn(d) if s else at_y(d)
-        return rc(c2_out.at[s, d], c2_in.at[s, d], c2_s.at[s, d], c2_r.at[s, d], dev)
-
-    for d in order:
-        for s in range(2):
-            for h in range(ZH):
-                c1_out[d, s, h] = routed(s, rep_of(h, (y + d) % Y, 1 - core)).astype(bf16)
-        go(c1_copy(d))
-    for d in order:
-        c1_copy(d).wait_recv()
-        for s in (1, 0):
-            for h in range(ZH):
-                both = routed(s, rep_of(h, (y + d) % Y, core)) + c1_in[d, s, h].astype(f32)
+        i = (h, s, d)
+        return rc(c2_out.at[i], c2_in.at[i], c2_s.at[i], c2_r.at[i], dev)
+
+    def c3_copy(h):
+        return rc(c3_out.at[h], c3_in.at[h], c3_s.at[h], c3_r.at[h], (b, r_oz))
+
+    for h in range(ZH):
+        for d in order:
+            for s in range(2):
+                c1_out[h, d, s] = routed(s, rep_of(h, (y + d) % Y, 1 - core)).astype(bf16)
+            go(c1_copy(h, d))
+    for h in range(ZH):
+        for d in order:
+            c1_copy(h, d).wait_recv()
+            for s in (1, 0):
+                both = routed(s, rep_of(h, (y + d) % Y, core)) + c1_in[h, d, s].astype(f32)
                 if s or d:
-                    c2_out[s, d, h] = both.astype(bf16)
+                    c2_out[h, s, d] = both.astype(bf16)
+                    go(c2_copy(h, s, d))
                 else:
                     part[h] = both
-            if s or d:
-                go(c2_copy(s, d))
-
-    for s in range(2):
-        for d in range(1 - s, Y):
-            c2_copy(s, d).wait_recv()
     for h in range(ZH):
         t = part[h]
         for s in range(2):
             for d in range(1 - s, Y):
-                t = t + c2_in[s, d, h].astype(f32)
+                c2_copy(h, s, d).wait_recv()
+                t = t + c2_in[h, s, d].astype(f32)
         part[h] = t
         c3_out[h] = t.astype(bf16)
-
-    def c3_copy():
-        return rc(c3_out, c3_in, c3_s, c3_r, (b, r_oz))
-
-    go(c3_copy())
+        go(c3_copy(h))
+    flush(ZH)
     up_copy().wait_recv()
-    c3_copy().wait_recv()
 
     def place(s, h, v, c):
         return ((c * Y + v) * 2 + s) * ZH + h
 
+    def tile(s, h, v, c):
+        return slopes.at[place(s, h, v, c)]
+
+    def e2_copy(h, s, d):
+        dev = at_up(d) if s else at_y(d)
+        own = tile(0, h, y, core)
+        return rc(own, tile(s, h, y, core), e2_s.at[h, s, d], e2_r.at[h, s, d], dev)
+
+    def e3_copy(h, s, d, c):
+        got = tile(s, h, (y + Y - d) % Y, c)
+        return rc(got, got, e3_s.at[h, s, d], e3_r.at[h, s, d], sib)
+
+    w = weight[...]
     for h in range(ZH):
-        summed = part[h] + c3_in[h].astype(f32)
+        c3_copy(h).wait_recv()
+        gathered = part[h] + c3_in[h].astype(f32)
+        high = gathered.astype(bf16)
+        low = (gathered - high.astype(f32)).astype(bf16)
+        tops[h] = high
+        summed = dot(high, w) + dot(low, w)
         sig = jax.nn.sigmoid(summed)
         given = jnp.where(zh == h, up[...], up_far[...]).astype(f32)
         slope = given * (sig * (1.0 + summed * (1.0 - sig)))
         slopes[place(0, h, y, core)] = slope.T.astype(bf16)
+        for d in order:
+            go(e2_copy(h, 1, d))
+            if d:
+                go(e2_copy(h, 0, d))
+        go(e3_copy(h, 0, 0, core))
         part[h] = summed * sig
-
-    def pair(s, v, c):
-        return slopes.at[pl.ds(place(s, 0, v, c), ZH)]
-
-    def e2_copy(s, d):
-        dev = at_up(d) if s else at_y(d)
-        own = pair(0, y, core)
-        return rc(own, pair(s, y, core), e2_s.at[s, d], e2_r.at[s, d], dev)
-
-    def e3_copy(s, d, c):
-        got = pair(s, (y + Y - d) % Y, c)
-        return rc(got, got, e3_s.at[s, d], e3_r.at[s, d], sib)
-
-    for d in order:
-        go(e2_copy(1, d))
-        if d:
-            go(e2_copy(0, d))
-    go(e3_copy(0, 0, core))
     hidden[...] = part[zh].astype(bf16)
-    for d in (0,) + order[:-1]:
+
+    U = T // (2 * Y)
+    total = dot(slopes[place(0, zh, y, core)], tops[zh])
+    wg_out[...] = total.reshape(2 * Y, U, T)
+
+    def h0_copy():
+        return rc(wg_out.at[pl.ds((1 - core) * Y, Y)], h0_in, h0_s, h0_r, sib)
+
+    go(h0_copy())
+
+    for h in range(ZH):
+        for d in (0,) + order[:-1]:
+            for s in range(2):
+                if s or d:
+                    e2_copy(h, s, d).wait_recv()
+                    go(e3_copy(h, s, d, core))
+
+    def h1_copy(d):
+        return rc(halves.at[(y + d) % Y], h1_in.at[d], h1_s.at[d], h1_r.at[d], at_y(d))
+
+    h0_copy().wait_recv()
+    halves[...] = wg_out[pl.ds(core * Y, Y)] + h0_in[...]
+    for d in range(1, Y):
+        go(h1_copy(d))
+
+    flush(2 * Y)
+    for h in range(ZH):
         for s in range(2):
-            if s or d:
-                e2_copy(s, d).wait_recv()
-                go(e3_copy(s, d, core))
-    for s in range(2):
-        for d in range(Y):
-            e3_copy(s, d, 1 - core).wait_recv()
+            for d in range(Y):
+                e3_copy(h, s, d, 1 - core).wait_recv()
+
+    zz = zh * ZL + z
+
+    def h2_copy(i, to):
+        h, d = (zh + i // ZL) % ZH, i % ZL
+        v = (z + (d if to else ZL - d)) % ZL
+        slot = h2_buf.at[zz] if to else h2_buf.at[h * ZL + v]
+        dev = (x * ZL + v, rep_of(h, y, core))
+        return rc(slot, slot, h2_s.at[i], h2_r.at[i], dev)
+
+    unit = halves[y]
+    for d in range(1, Y):
+        h1_copy(d).wait_recv()
+        unit = unit + h1_in[d]
+    h2_buf[zz] = unit.astype(bf16)
+    for i in range(1, ZH * ZL):
+        go(h2_copy(i, True))
 
     def backward(n):
         out = None
@@ -384,28 +429,18 @@
             out = term if out is None else out + term
         out = out.astype(bf16)
         terms[n] = out
-        return dot(out, feats[n])
 
     def gx_copy(k, e):
         first = ((x + e) % X) * ZL + (ohalf, half)[k] * ZQ
         return rc(terms.at[pl.ds(first, ZQ)], gx_in.at[k, e], gx_s.at[k, e], gx_r.at[k, e], at_x(e))
 
-    total = jnp.zeros((T, T), f32)
     for k in range(2):
         for e in tuple(range(1, X)) + (0,):
             first = ((x + e) % X) * ZL + (ohalf, half)[k] * ZQ
             for i in range(ZQ):
-                total = total + backward(first + i)
+                backward(first + i)
             if e:
                 go(gx_copy(k, e))
-
-    U = T // (2 * Y)
-    wg_out[...] = total.reshape(2 * Y, U, T)
-
-    def h0_copy():
-        return rc(wg_out.at[pl.ds((1 - core) * Y, Y)], h0_in, h0_s, h0_r, sib)
-
-    go(h0_copy())
 
     def gx_sum(k, v):
         t = terms[x * ZL + (ohalf, half)[k] * ZQ + v].astype(f32)
@@ -431,46 +466,7 @@
             go(gz_copy(k, m))
         return gx_sum(k, zq)
 
-    def h1_copy(d):
-        return rc(halves.at[(y + d) % Y], h1_in.at[d], h1_s.at[d], h1_r.at[d], at_y(d))
-
-    h0_copy().wait_recv()
-    halves[...] = wg_out[pl.ds(core * Y, Y)] + h0_in[...]
-    for d in range(1, Y):
-        go(h1_copy(d))
-
     crossing = gx_wait(0)
-
-    zz = zh * ZL + z
-
-    def h2_copy(i, to):
-        h, d = (zh + i // ZL) % ZH, i % ZL
-        v = (z + (d if to else ZL - d)) % ZL
-        slot = h2_buf.at[zz] if to else h2_buf.at[h * ZL + v]
-        dev = (x * ZL + v, rep_of(h, y, core))
-        return rc(slot, slot, h2_s.at[i], h2_r.at[i], dev)
-
-    unit = halves[y]
-    for d in range(1, Y):
-        h1_copy(d).wait_recv()
-        unit = unit + h1_in[d]
-    h2_buf[zz] = unit.astype(bf16)
-    for i in range(1, ZH * ZL):
-        go(h2_copy(i, True))
-
-    kept = gx_wait(1)
-
-    def gz2_copy():
-        return rc(gz2_out, gz2_in, gz2_s, gz2_r, (x * ZL + ohalf * ZQ + zq, r))
-
-    for m in range(1, ZQ):
-        gz_copy(0, m).wait_recv()
-        crossing = crossing + gz_in[0, m].astype(f32)
-    gz2_out[...] = crossing.astype(bf16)
-    go(gz2_copy())
-    for m in range(1, ZQ):
-        gz_copy(1, m).wait_recv()
-        kept = kept + gz_in[1, m].astype(f32)
 
     def h3_copy(e, v):
         return rc(h3_buf.at[v], h3_buf.at[v], h3_s.at[e], h3_r.at[e], at_x(e))
@@ -484,11 +480,7 @@
     for e in range(1, X):
         go(h3_copy(e, x))
 
-    gz2_copy().wait_recv()
-    pulled = (kept + gz2_in[...].astype(f32)).T.astype(bf16)
-    input_grad[...] = lax.dot_general(
-        pulled, w, (((1,), (1,)), ((), ())), preferred_element_type=f32
-    ).astype(bf16)
+    kept = gx_wait(1)
 
     def h4_copy(d, v):
         slot = wg_all.at[core * Y + v]
@@ -507,15 +499,35 @@
     for d in range(1, Y):
         go(h4_copy(d, y))
     go(h5_copy(0, core))
+
+    def gz2_copy():
+        return rc(gz2_out, gz2_in, gz2_s, gz2_r, (x * ZL + ohalf * ZQ + zq, r))
+
+    for m in range(1, ZQ):
+        gz_copy(0, m).wait_recv()
+        crossing = crossing + gz_in[0, m].astype(f32)
+    gz2_out[...] = crossing.astype(bf16)
+    go(gz2_copy())
+    for m in range(1, ZQ):
+        gz_copy(1, m).wait_recv()
+        kept = kept + gz_in[1, m].astype(f32)
+
+    flush(1)
     for d in range(1, Y):
         h4_copy(d, (y + Y - d) % Y).wait_recv()
         go(h5_copy(d, core))
+
     for d in range(Y):
         h5_copy(d, 1 - core).wait_recv()
     weight_grad[...] = wg_all[...].reshape(T, T).T
 
-    for copy in sends:
-        copy.wait_send()
+    gz2_copy().wait_recv()
+    pulled = (kept + gz2_in[...].astype(f32)).T.astype(bf16)
+    input_grad[...] = lax.dot_general(
+        pulled, w, (((1,), (1,)), ((), ())), preferred_element_type=f32
+    ).astype(bf16)
+
+    flush(0)
 
 
 def local(features, weight, adjacency, row_tiles, live_counts, upstream):
@@ -542,11 +554,12 @@
         pltpu.SMEM((16, T), jnp.int32),
         buf(BLK, T),
         buf(4 * BLK + 1, T, dtype=f32),
-        buf(Y, 2, ZH, T),
-        buf(Y, 2, ZH, T),
-        buf(2, Y, ZH, T),
-        buf(2, Y, ZH, T),
+        buf(ZH, Y, 2, T),
+        buf(ZH, Y, 2, T),
+        buf(ZH, 2, Y, T),
+        buf(ZH, 2, Y, T),
         buf(ZH, T, dtype=f32),
+        buf(ZH, T),
         buf(ZH, T),
         buf(ZH, T),
         buf(2 * REP + 1, T),
@@ -570,16 +583,16 @@
         dma((X, ZL)),
         dma,
         dma,
-        dma((Y,)),
-        dma((Y,)),
-        dma((2, Y)),
-        dma((2, Y)),
-        dma,
-        dma,
-        dma((2, Y)),
-        dma((2, Y)),
-        dma((2, Y)),
-        dma((2, Y)),
+        dma((ZH, Y)),
+        dma((ZH, Y)),
+        dma((ZH, 2, Y)),
+        dma((ZH, 2, Y)),
+        dma((ZH,)),
+        dma((ZH,)),
+        dma((ZH, 2, Y)),
+        dma((ZH, 2, Y)),
+        dma((ZH, 2, Y)),
+        dma((ZH, 2, Y)),
         dma((2, X)),
         dma((2, X)),
         dma((2, ZQ)),

time: 101 us -> 86.1 us (0.85)
  Pallas kernels: 98.6 us -> 83.5 us
    pallas_call x1, Pallas kernels: 98.6 us -> 83.5 us  [local(): pl.pallas_call(kernel, name='graph_layer', out_shape=(jax.ShapeDtypeStruc...]
where the time goes in v5:
time: 86.1 us; the launch traced here: 86 us
  Pallas kernels  83.5 us (97%)
  local copies, waits for them, and re-layouts  1.86 us (2%)
    pallas_call x1, Pallas kernels, local(): pl.pallas_call(kernel, name='graph_layer', out_shape=(jax.ShapeDtypeStruc...  83.5 us
    unnamed x3, local copies, waits for them, and re-layouts  1.86 us

profile of v5, /device:TPU:1, one launch (start us, length us, event | category | flops | bytes accessed | tf_op | source)
XLA Modules:
  0.0 86.0 jit_solution(17696262126125621212)
XLA Ops:
  0.6 83.5 %graph_layer.1 = (bf16[128,128]{1,0:T(8,128)(2,1)S(1)}, bf16[128,128]{1,0:T(8,128)(2,1)S(1)}, f32[128,128]{1,0:T(8,128)S(1)}) custom-call(bf16[128,128]{1,0:T(8,128)(2,1)} %feat_hbm.1, bf16[128,128]{1,0:T(8,128)(2,1)} %weight_hbm.1, bf16[128,128]{1,0:T(8,128)(2,1)} %up_hbm.1, bf16[128,128,128]{2,1,0:T(8,128)(2,1)} %bitcast.5, s32[2,2,32]{2,1,0:T(2,128)} %bitcast.6, ...), custom_call_target="tpu_custom_call" | custom-call | tf_op jit(solution)/shard_map/graph_layer/pallas_call | solution.py:615
  84.2 0.6 copy.12
  84.8 0.6 copy.13
  85.4 0.6 copy.14

commit v6 on v5

--- a/solution.py
+++ b/solution.py
@@ -47,6 +47,7 @@
     tops,
     slopes,
     terms,
+    gx_out,
     gx_in,
     gz_out,
     gz_in,
@@ -154,7 +155,7 @@
     def greet(dev):
         pl.semaphore_signal(bar, inc=1, device_id=dev, device_id_type=MESH)
 
-    for i in range(1, ZH * ZL):
+    for i in reversed(range(1, ZH * ZL)):
         greet((x * ZL + (z + i % ZL) % ZL, rep_of((zh + i // ZL) % ZH, y, core)))
     for d in range(1, X):
         greet(at_x(d))
@@ -167,6 +168,50 @@
 
     half, zq = z // ZQ, z % ZQ
     ohalf = 1 - half
+
+    sums[2 * SL] = jnp.zeros((T, T), f32)
+    slopes[2 * REP] = jnp.zeros((T, T), bf16)
+    in_copies[0].wait()
+
+    sends = []
+
+    def go(copy):
+        copy.start()
+        sends.append(copy)
+        return copy
+
+    def flush(keep):
+        done = sends[: len(sends) - keep]
+        del sends[: len(done)]
+        for copy in done:
+            copy.wait_send()
+
+    pl.semaphore_wait(bar, (ZH * ZL - 1) + (X - 1) + (Y - 1) + 1 + 2 * Y)
+
+    def zsrc(g):
+        return (half, ohalf)[g // ZQ] * ZQ + (zq + ZQ - g % ZQ) % ZQ
+
+    def mate(m):
+        return (x * ZL + half * ZQ + (zq + m) % ZQ, r)
+
+    partner = (x * ZL + ohalf * ZQ + zq, r)
+
+    def az_copy(g, v, dev):
+        slot = feats.at[x * ZL + v]
+        return rc(slot, slot, az_s.at[g], az_r.at[g], dev)
+
+    def ax_copy(g, e, v):
+        slot = feats.at[v * ZL + zsrc(g)]
+        return rc(slot, slot, ax_s.at[e, g], ax_r.at[e, g], at_x(e))
+
+    def along_x(g):
+        for e in range(1, X):
+            go(ax_copy(g, e, x))
+
+    go(az_copy(ZQ, z, partner))
+    for m in range(1, ZQ):
+        go(az_copy(m, z, mate(m)))
+    along_x(0)
 
     in_copies[1].wait()
     in_copies[2].wait()
@@ -204,7 +249,7 @@
                 for o in range(2)
             ]
             tab_v[2 * s + k : 2 * s + k + 1, :BLK] = best(hits)
-            spot = ((((row_l & 1) * Y + ((row_l // 2) & (Y - 1))) * 2 + s) * ZH) + row_l // (2 * Y)
+            spot = (((row_l & 1) * Y + ((row_l // 2) & (Y - 1))) * ZH + row_l // (2 * Y)) * 2 + s
             tab_v[6 + 2 * s + k : 7 + 2 * s + k, :BLK] = jnp.where(live_l > k, spot, 2 * REP)
         hits = [
             jnp.where((row_s[o] == t_l) & (live_s > o), code[o][:, :1], -1) for o in range(2)
@@ -212,50 +257,7 @@
         tab_v[4 + s : 5 + s, :REP] = best(hits)
     to_scalars = pltpu.make_async_copy(tab_v, table, in_sem.at[6])
     to_scalars.start()
-    sums[2 * SL] = jnp.zeros((T, T), f32)
-    slopes[2 * REP] = jnp.zeros((T, T), bf16)
-    in_copies[0].wait()
-    in_copies[3].wait()
-
-    sends = []
-
-    def go(copy):
-        copy.start()
-        sends.append(copy)
-        return copy
-
-    def flush(keep):
-        done = sends[: len(sends) - keep]
-        del sends[: len(done)]
-        for copy in done:
-            copy.wait_send()
-
-    pl.semaphore_wait(bar, (ZH * ZL - 1) + (X - 1) + (Y - 1) + 1 + 2 * Y)
-
-    def zsrc(g):
-        return (half, ohalf)[g // ZQ] * ZQ + (zq + ZQ - g % ZQ) % ZQ
-
-    def mate(m):
-        return (x * ZL + half * ZQ + (zq + m) % ZQ, r)
-
-    partner = (x * ZL + ohalf * ZQ + zq, r)
-
-    def az_copy(g, v, dev):
-        slot = feats.at[x * ZL + v]
-        return rc(slot, slot, az_s.at[g], az_r.at[g], dev)
-
-    def ax_copy(g, e, v):
-        slot = feats.at[v * ZL + zsrc(g)]
-        return rc(slot, slot, ax_s.at[e, g], ax_r.at[e, g], at_x(e))
-
-    def along_x(g):
-        for e in range(1, X):
-            go(ax_copy(g, e, x))
-
-    go(az_copy(ZQ, z, partner))
-    for m in range(1, ZQ):
-        go(az_copy(m, z, mate(m)))
-    along_x(0)
+
     for m in range(1, ZQ):
         az_copy(m, zsrc(m), mate(m)).wait_recv()
         along_x(m)
@@ -337,7 +339,7 @@
     up_copy().wait_recv()
 
     def place(s, h, v, c):
-        return ((c * Y + v) * 2 + s) * ZH + h
+        return ((c * Y + v) * ZH + h) * 2 + s
 
     def tile(s, h, v, c):
         return slopes.at[place(s, h, v, c)]
@@ -347,10 +349,11 @@
         own = tile(0, h, y, core)
         return rc(own, tile(s, h, y, core), e2_s.at[h, s, d], e2_r.at[h, s, d], dev)
 
-    def e3_copy(h, s, d, c):
-        got = tile(s, h, (y + Y - d) % Y, c)
-        return rc(got, got, e3_s.at[h, s, d], e3_r.at[h, s, d], sib)
-
+    def e3_copy(h, d, c):
+        both = slopes.at[pl.ds(place(0, h, (y + Y - d) % Y, c), 2)]
+        return rc(both, both, e3_s.at[h, d], e3_r.at[h, d], sib)
+
+    in_copies[3].wait()
     w = weight[...]
     for h in range(ZH):
         c3_copy(h).wait_recv()
@@ -367,7 +370,6 @@
             go(e2_copy(h, 1, d))
             if d:
                 go(e2_copy(h, 0, d))
-        go(e3_copy(h, 0, 0, core))
         part[h] = summed * sig
     hidden[...] = part[zh].astype(bf16)
 
@@ -380,26 +382,22 @@
 
     go(h0_copy())
 
-    for h in range(ZH):
+    def h1_copy(d):
+        return rc(halves.at[(y + d) % Y], h1_in.at[d], h1_s.at[d], h1_r.at[d], at_y(d))
+
+    h0_copy().wait_recv()
+    halves[...] = wg_out[pl.ds(core * Y, Y)] + h0_in[...]
+    for d in range(1, Y):
+        go(h1_copy(d))
+
+    def to_sibling(h):
         for d in (0,) + order[:-1]:
             for s in range(2):
                 if s or d:
                     e2_copy(h, s, d).wait_recv()
-                    go(e3_copy(h, s, d, core))
-
-    def h1_copy(d):
-        return rc(halves.at[(y + d) % Y], h1_in.at[d], h1_s.at[d], h1_r.at[d], at_y(d))
-
-    h0_copy().wait_recv()
-    halves[...] = wg_out[pl.ds(core * Y, Y)] + h0_in[...]
-    for d in range(1, Y):
-        go(h1_copy(d))
-
-    flush(2 * Y)
-    for h in range(ZH):
-        for s in range(2):
-            for d in range(Y):
-                e3_copy(h, s, d, 1 - core).wait_recv()
+            go(e3_copy(h, d, core))
+
+    to_sibling(0)
 
     zz = zh * ZL + z
 
@@ -417,6 +415,14 @@
     h2_buf[zz] = unit.astype(bf16)
     for i in range(1, ZH * ZL):
         go(h2_copy(i, True))
+
+    for h in range(1, ZH):
+        to_sibling(h)
+
+    flush(Y)
+    for h in range(ZH):
+        for d in range(Y):
+            e3_copy(h, d, 1 - core).wait_recv()
 
     def backward(n):
         out = None
@@ -430,23 +436,55 @@
         out = out.astype(bf16)
         terms[n] = out
 
-    def gx_copy(k, e):
-        first = ((x + e) % X) * ZL + (ohalf, half)[k] * ZQ
-        return rc(terms.at[pl.ds(first, ZQ)], gx_in.at[k, e], gx_s.at[k, e], gx_r.at[k, e], at_x(e))
-
+    ZP = ZQ // 2
+    turn_x, mirror_x = x + 1 - 2 * (x % 2), X - 1 - x
+    over_x = (x + X // 2) % X
+    meets = ((turn_x, mirror_x), (mirror_x, turn_x))
+
+    def spot_of(v, k, g):
+        return v * ZL + (ohalf, half)[k] * ZQ + g * ZP
+
+    def gx_copy(k, g, step):
+        to = (meets[g][step // 2] * ZL + z, r)
+        i = (k, g, step)
+        if step == 2:
+            src = gx_out.at[k, g]
+        else:
+            src = terms.at[pl.ds(spot_of((over_x, meets[g][0])[step], k, g), ZP)]
+        return rc(src, gx_in.at[i], gx_s.at[i], gx_r.at[i], to)
+
+    def column_tiles(v, k):
+        for g in range(2):
+            for i in range(ZP):
+                backward(spot_of(v[g], k, g) + i)
+
+    def first_step(k, step):
+        column_tiles(((over_x, over_x), (turn_x, mirror_x))[step], k)
+        for g in range(2):
+            go(gx_copy(k, g, step))
+
+    def second_step(k):
+        for g in range(2):
+            gx_copy(k, g, 0).wait_recv()
+            mine = terms[pl.ds(spot_of(meets[g][1], k, g), ZP)].astype(f32)
+            gx_out[k, g] = (mine + gx_in[k, g, 0].astype(f32)).astype(bf16)
+            go(gx_copy(k, g, 2))
+
+    first_step(0, 0)
+    first_step(0, 1)
+    first_step(1, 0)
     for k in range(2):
-        for e in tuple(range(1, X)) + (0,):
-            first = ((x + e) % X) * ZL + (ohalf, half)[k] * ZQ
-            for i in range(ZQ):
-                backward(first + i)
-            if e:
-                go(gx_copy(k, e))
+        column_tiles((mirror_x, turn_x), k)
+    second_step(0)
+    first_step(1, 1)
+    for k in range(2):
+        column_tiles((x, x), k)
+    second_step(1)
 
     def gx_sum(k, v):
-        t = terms[x * ZL + (ohalf, half)[k] * ZQ + v].astype(f32)
-        for e in range(1, X):
-            t = t + gx_in[k, e, v].astype(f32)
-        return t
+        g, i = v // ZP, v % ZP
+        t = terms[spot_of(x, k, 0) + v].astype(f32)
+        return t + gx_in[k, g, 1, i].astype(f32) + gx_in[k, g, 2, i].astype(f32)
 
     def gz_copy(k, m):
         v = (zq + m) % ZQ
@@ -459,8 +497,9 @@
         )
 
     def gx_wait(k):
-        for e in range(1, X):
-            gx_copy(k, e).wait_recv()
+        for g in range(2):
+            for step in (1, 2):
+                gx_copy(k, g, step).wait_recv()
         for m in range(1, ZQ):
             gz_out[k, m] = gx_sum(k, (zq + m) % ZQ).astype(bf16)
             go(gz_copy(k, m))
@@ -564,7 +603,8 @@
         buf(ZH, T),
         buf(2 * REP + 1, T),
         buf(BLK, T),
-        buf(2, X, ZQ, T),
+        buf(2, 2, ZQ // 2, T),
+        buf(2, 2, 3, ZQ // 2, T),
         buf(2, ZQ, T),
         buf(2, ZQ, T),
         buf(T),
@@ -591,10 +631,10 @@
         dma((ZH,)),
         dma((ZH, 2, Y)),
         dma((ZH, 2, Y)),
-        dma((ZH, 2, Y)),
-        dma((ZH, 2, Y)),
-        dma((2, X)),
-        dma((2, X)),
+        dma((ZH, Y)),
+        dma((ZH, Y)),
+        dma((2, 2, 3)),
+        dma((2, 2, 3)),
         dma((2, ZQ)),
         dma((2, ZQ)),
         dma,

time: 86.1 us -> 83.3 us (0.967); the launches traced: 86 us -> 82 us
  Pallas kernels: 83.5 us -> 79.5 us
    pallas_call x1, Pallas kernels: 83.5 us -> 79.5 us  [local(): pl.pallas_call(kernel, name='graph_layer', out_shape=(jax.ShapeDtypeStruc...]
where the time goes in v6:
time: 83.3 us; the launch traced here: 82 us
  Pallas kernels  79.5 us (95%)
  local copies, waits for them, and re-layouts  1.86 us (2%)
    pallas_call x1, Pallas kernels, local(): pl.pallas_call(kernel, name='graph_layer', out_shape=(jax.ShapeDtypeStruc...  79.5 us
    unnamed x3, local copies, waits for them, and re-layouts  1.86 us

profile of v6, /device:TPU:1, one launch (start us, length us, event | category | flops | bytes accessed | tf_op | source)
XLA Modules:
  0.0 82.0 jit_solution(1141401672790272084)
XLA Ops:
  0.6 79.5 %graph_layer.1 = (bf16[128,128]{1,0:T(8,128)(2,1)S(1)}, bf16[128,128]{1,0:T(8,128)(2,1)S(1)}, f32[128,128]{1,0:T(8,128)S(1)}) custom-call(bf16[128,128]{1,0:T(8,128)(2,1)} %feat_hbm.1, bf16[128,128]{1,0:T(8,128)(2,1)} %weight_hbm.1, bf16[128,128]{1,0:T(8,128)(2,1)} %up_hbm.1, bf16[128,128,128]{2,1,0:T(8,128)(2,1)} %bitcast.5, s32[2,2,32]{2,1,0:T(2,128)} %bitcast.6, ...), custom_call_target="tpu_custom_call" | custom-call | tf_op jit(solution)/shard_map/graph_layer/pallas_call | solution.py:655
  80.2 0.6 copy.12
  80.8 0.6 copy.13
  81.4 0.6 copy.14

commit v7 on v6

--- a/solution.py
+++ b/solution.py
@@ -60,6 +60,7 @@
     h2_buf,
     h3_buf,
     wg_all,
+    ring_sem,
     in_sem,
     az_s,
     az_r,
@@ -126,6 +127,10 @@
     def at_up(d):
         return (b_up, rep_of((zh + last) % ZH, (y + d) % Y, core))
 
+    def at_ring(i):
+        v = (zh * ZL + z + i) % (ZH * ZL)
+        return (x * ZL + v % ZL, rep_of(v // ZL, y, core))
+
     sib = (b, rep_of(zh, y, 1 - core))
     r_oz = rep_of(ozh, y, core)
 
@@ -155,8 +160,9 @@
     def greet(dev):
         pl.semaphore_signal(bar, inc=1, device_id=dev, device_id_type=MESH)
 
-    for i in reversed(range(1, ZH * ZL)):
-        greet((x * ZL + (z + i % ZL) % ZL, rep_of((zh + i // ZL) % ZH, y, core)))
+    for i in range(ZQ, 0, -1):
+        greet(at_ring(i))
+        greet(at_ring(ZH * ZL - i))
     for d in range(1, X):
         greet(at_x(d))
     for d in range(1, Y):
@@ -186,7 +192,7 @@
         for copy in done:
             copy.wait_send()
 
-    pl.semaphore_wait(bar, (ZH * ZL - 1) + (X - 1) + (Y - 1) + 1 + 2 * Y)
+    pl.semaphore_wait(bar, 2 * ZQ + (X - 1) + (Y - 1) + 1 + 2 * Y)
 
     def zsrc(g):
         return (half, ohalf)[g // ZQ] * ZQ + (zq + ZQ - g % ZQ) % ZQ
@@ -212,6 +218,9 @@
     for m in range(1, ZQ):
         go(az_copy(m, z, mate(m)))
     along_x(0)
+
+    for i in (ZQ, ZH * ZL - ZQ):
+        pl.semaphore_signal(ring_sem, inc=1, device_id=at_ring(i), device_id_type=MESH)
 
     in_copies[1].wait()
     in_copies[2].wait()
@@ -281,7 +290,7 @@
                 sums[q] = prod[:T] + sums[table[2 * s, n]]
                 sums[q + 1] = prod[T:] + sums[table[2 * s + 1, n]]
 
-    early = ZQ - 1
+    early = ZQ // 2
     for g in range(early):
         forward(g)
     for m in range(1, ZQ):
@@ -297,8 +306,9 @@
         return rc(up, up_far, up_s, up_r, (b, r_oz))
 
     in_copies[5].wait()
+    pl.semaphore_wait(ring_sem, 2)
     go(up_copy())
-    order = tuple(range(1, Y)) + (0,)
+    order = tuple(sorted(range(1, Y), key=lambda d: -min(d, Y - d))) + (0,)
 
     def c1_copy(h, d):
         return rc(c1_out.at[h, d], c1_in.at[h, d], c1_s.at[h, d], c1_r.at[h, d], sib)
@@ -419,7 +429,6 @@
     for h in range(1, ZH):
         to_sibling(h)
 
-    flush(Y)
     for h in range(ZH):
         for d in range(Y):
             e3_copy(h, d, 1 - core).wait_recv()
@@ -505,6 +514,7 @@
             go(gz_copy(k, m))
         return gx_sum(k, zq)
 
+    flush(12)
     crossing = gx_wait(0)
 
     def h3_copy(e, v):
@@ -616,6 +626,7 @@
         buf(ZH * ZL, U),
         buf(X, U, dtype=f32),
         buf(2 * Y, U, dtype=f32),
+        pltpu.SemaphoreType.REGULAR,
         dma((7,)),
         dma((ZL,)),
         dma((ZL,)),

time: 83.3 us -> 81.9 us (0.983); the launches traced: 82 us -> 81.8 us
  no operation moved by 1% of the time
where the time goes in v7:
time: 81.9 us; the launch traced here: 81.8 us
  Pallas kernels  79.3 us (97%)
  local copies, waits for them, and re-layouts  1.86 us (2%)
    pallas_call x1, Pallas kernels, local(): pl.pallas_call(kernel, name='graph_layer', out_shape=(jax.ShapeDtypeStruc...  79.3 us
    unnamed x3, local copies, waits for them, and re-layouts  1.86 us

profile of v7, /device:TPU:1, one launch (start us, length us, event | category | flops | bytes accessed | tf_op | source)
XLA Modules:
  0.0 81.8 jit_solution(3387172898403653392)
XLA Ops:
  0.6 79.3 %graph_layer.1 = (bf16[128,128]{1,0:T(8,128)(2,1)S(1)}, bf16[128,128]{1,0:T(8,128)(2,1)S(1)}, f32[128,128]{1,0:T(8,128)S(1)}) custom-call(bf16[128,128]{1,0:T(8,128)(2,1)} %feat_hbm.1, bf16[128,128]{1,0:T(8,128)(2,1)} %weight_hbm.1, bf16[128,128]{1,0:T(8,128)(2,1)} %up_hbm.1, bf16[128,128,128]{2,1,0:T(8,128)(2,1)} %bitcast.5, s32[2,2,32]{2,1,0:T(2,128)} %bitcast.6, ...), custom_call_target="tpu_custom_call" | custom-call | tf_op jit(solution)/shard_map/graph_layer/pallas_call | solution.py:666
  79.9 0.6 copy.12
  80.6 0.6 copy.13
  81.2 0.6 copy.14

commit v8 on v7

--- a/solution.py
+++ b/solution.py
@@ -175,6 +175,14 @@
     half, zq = z // ZQ, z % ZQ
     ohalf = 1 - half
 
+    def other(m):
+        v, bit = zq, 1
+        while bit <= m:
+            if m & bit:
+                v = v + bit - 2 * bit * ((zq // bit) % 2)
+            bit *= 2
+        return v
+
     sums[2 * SL] = jnp.zeros((T, T), f32)
     slopes[2 * REP] = jnp.zeros((T, T), bf16)
     in_copies[0].wait()
@@ -195,10 +203,10 @@
     pl.semaphore_wait(bar, 2 * ZQ + (X - 1) + (Y - 1) + 1 + 2 * Y)
 
     def zsrc(g):
-        return (half, ohalf)[g // ZQ] * ZQ + (zq + ZQ - g % ZQ) % ZQ
+        return (half, ohalf)[g // ZQ] * ZQ + other(g % ZQ)
 
     def mate(m):
-        return (x * ZL + half * ZQ + (zq + m) % ZQ, r)
+        return (x * ZL + half * ZQ + other(m), r)
 
     partner = (x * ZL + ohalf * ZQ + zq, r)
 
@@ -211,7 +219,7 @@
         return rc(slot, slot, ax_s.at[e, g], ax_r.at[e, g], at_x(e))
 
     def along_x(g):
-        for e in range(1, X):
+        for e in sorted(range(1, X), key=lambda e: min(e, X - e)):
             go(ax_copy(g, e, x))
 
     go(az_copy(ZQ, z, partner))
@@ -229,7 +237,7 @@
 
     def rank(n):
         far = ((n // ZQ) % 2) ^ half
-        return (far * ZQ + ((zq - n % ZQ) & (ZQ - 1))) * X + ((x - n // ZL) & (X - 1))
+        return (far * ZQ + (zq ^ (n % ZQ))) * X + ((x - n // ZL) & (X - 1))
 
     rank_s, rank_l = rank(i_s), rank(i_l)
 
@@ -496,7 +504,7 @@
         return t + gx_in[k, g, 1, i].astype(f32) + gx_in[k, g, 2, i].astype(f32)
 
     def gz_copy(k, m):
-        v = (zq + m) % ZQ
+        v = other(m)
         return rc(
             gz_out.at[k, m],
             gz_in.at[k, m],
@@ -510,7 +518,7 @@
             for step in (1, 2):
                 gx_copy(k, g, step).wait_recv()
         for m in range(1, ZQ):
-            gz_out[k, m] = gx_sum(k, (zq + m) % ZQ).astype(bf16)
+            gz_out[k, m] = gx_sum(k, other(m)).astype(bf16)
             go(gz_copy(k, m))
         return gx_sum(k, zq)
 

time: 81.9 us -> 81.4 us (level)
  no operation moved by 1% of the time
where the time goes in v8:
time: 81.4 us; the launch traced here: 81.3 us
  Pallas kernels  78.8 us (97%)
  local copies, waits for them, and re-layouts  1.86 us (2%)
    pallas_call x1, Pallas kernels, local(): pl.pallas_call(kernel, name='graph_layer', out_shape=(jax.ShapeDtypeStruc...  78.8 us
    unnamed x3, local copies, waits for them, and re-layouts  1.86 us

profile of v8, /device:TPU:1, one launch (start us, length us, event | category | flops | bytes accessed | tf_op | source)
XLA Modules:
  0.0 81.3 jit_solution(16028557212959696865)
XLA Ops:
  0.6 78.8 %graph_layer.1 = (bf16[128,128]{1,0:T(8,128)(2,1)S(1)}, bf16[128,128]{1,0:T(8,128)(2,1)S(1)}, f32[128,128]{1,0:T(8,128)S(1)}) custom-call(bf16[128,128]{1,0:T(8,128)(2,1)} %feat_hbm.1, bf16[128,128]{1,0:T(8,128)(2,1)} %weight_hbm.1, bf16[128,128]{1,0:T(8,128)(2,1)} %up_hbm.1, bf16[128,128,128]{2,1,0:T(8,128)(2,1)} %bitcast.5, s32[2,2,32]{2,1,0:T(2,128)} %bitcast.6, ...), custom_call_target="tpu_custom_call" | custom-call | tf_op jit(solution)/shard_map/graph_layer/pallas_call | solution.py:674
  79.4 0.6 copy.12
  80.0 0.6 copy.13
  80.6 0.6 copy.14
